TPU v7x, 256 devices: a whole 4x4x8 slice. The times are simulated.
256 devices in a mesh: seq: 16 (over z_hi, y, core), pipe: 16 (over x, z_lo).
Axes of the slice: x: 4, y: 4, z: 8 (z_hi: 2, z_lo: 4; z = z_hi * 4 + z_lo), core: 2. Of those that a mesh axis runs over, the one named last changes fastest.
Arguments:
- acts: bfloat16 [16, 2048, 2048], P('pipe', 'seq'), may hold values from -6 to 6
- norm_gain: float32 [16, 2048], P('pipe'), may hold values from 0.25 to 1.75
- query_weight: bfloat16 [16, 2048, 2048], P('pipe', None, 'seq'), may hold values from -64 to 64
- kv_weight: bfloat16 [16, 2048, 1024], P('pipe', None, 'seq'), may hold values from -64 to 64
- out_weight: bfloat16 [16, 2048, 2048], P('pipe', 'seq'), may hold values from -0.125 to 0.125
- first_values: bfloat16 [16, 2048, 512], P('pipe', 'seq'), may hold values from -6 to 6
- mix_weight: float32 [16, 8], P('pipe'), may hold values from 0.2 to 0.8
Outputs:
- passed: bfloat16 [16, 2048, 2048], P('pipe', 'seq')
- fresh_values: bfloat16 [16, 2048, 512], P('pipe', 'seq')
All inputs are finite; a program needn't handle non-finite values.
Results may differ from a plain program's by a relative error of at most 0.011.
Values may be sent and summed in bfloat16 or wider, within the bound.
No kernel may reach another device: no remote copies, remote signals or barrier semaphores. Data moves between devices by JAX's collectives and lax.ppermute only.
A program may use at most 128 MiB of HBM per device.

v0:
```python
import functools

import jax
import jax.numpy as jnp
from jax import lax
from jax.experimental import pallas as pl
from jax.experimental.pallas import tpu as pltpu
from jax.sharding import Mesh
from jax.sharding import PartitionSpec as P

HALVES, RING, CORES, XS, ZS = 2, 4, 2, 4, 4
SEQ = ("zh", "y", "c")
PIPE = ("x", "zl")
rope_base = 500000.0
F32 = jnp.float32
BF16 = jnp.bfloat16
CHUNK = 512


def prepare_kernel(acts, gain, first, out):
    wide = acts[...].astype(F32)
    scale = lax.rsqrt(jnp.mean(wide * wide, axis=-1, keepdims=True) + 1e-05)
    normed = (wide * scale * gain[...]).astype(BF16)
    lanes = lax.broadcasted_iota(jnp.int32, (acts.shape[0], 128), 1)
    for to in range(RING):
        out[to, :, :2048] = normed
        at = to // 2 * 128
        low = first[:, at : at + 128].astype(F32)
        high = first[:, 256 + at : 384 + at].astype(F32)
        if to % 2 == 0:
            high = pltpu.roll(high, 64, 1)
        else:
            low = pltpu.roll(low, 64, 1)
        out[to, :, 2048:] = jnp.where(lanes < 64, low, high).astype(BF16)


def pull(x, axis, by):
    n = lax.axis_size(axis)
    return lax.ppermute(x, axis, [((i + by) % n, i) for i in range(n)])


def rope_tables(positions, head_dim):
    half = head_dim // 2
    freq = rope_base ** (-2.0 * jnp.arange(half, dtype=F32) / head_dim)
    angle = positions.astype(F32)[:, None] * freq
    cosine, sine = jnp.cos(angle), jnp.sin(angle)
    return (
        jnp.concatenate([cosine] * 4, axis=-1),
        jnp.concatenate([-sine, sine, -sine, sine], axis=-1),
    )


def rope(u, cosine, sine):
    lanes = lax.broadcasted_iota(jnp.int32, u.shape, 1)
    swapped = jnp.where(lanes % 64 < 32, pltpu.roll(u, 96, 1), pltpu.roll(u, 32, 1))
    return u * cosine + swapped * sine


def keyval_kernel(place, x, mine, theirs, cos, sin, mix, *refs):
    kv_out, val_out, w = refs[-3:]
    h, c, section = place[1], place[2], place[3]
    w[0:64], w[64:128], w[128:192], w[192:256] = mine[0:64], theirs[0:64], mine[64:128], theirs[64:128]
    both = lax.dot_general(x[:, :2048], w[...], (((1,), (1,)), ((), ())), preferred_element_type=F32)
    rows = 128
    for slot in range(RING):
        part = both[slot * rows : (slot + 1) * rows]
        own, other = part[:, :128], part[:, 128:]
        keys = jnp.where(h == 0, own, other)
        values = jnp.where(h == 0, other, own)
        keys = jnp.where(c == 0, keys, pltpu.roll(keys, 64, 1))
        values = jnp.where(c == 0, values, pltpu.roll(values, 64, 1))
        rounded = values.astype(BF16)
        wide = rounded.astype(F32)
        before = jnp.where(section == 0, wide, x[slot * rows : (slot + 1) * rows, 2048:].astype(F32))
        mixed = mix[0:1, :] * wide + (1.0 - mix[0:1, :]) * before
        keys = rope(keys, cos[slot], sin[slot])
        lanes = lax.broadcasted_iota(jnp.int32, keys.shape, 1)
        low = jnp.where(lanes < 64, keys, pltpu.roll(mixed, 64, 1))
        high = jnp.where(lanes < 64, pltpu.roll(keys, 64, 1), mixed)
        kv_out[slot, :, 0:128] = low.astype(BF16)
        kv_out[slot, :, 128:256] = high.astype(BF16)
        val_out[slot] = rounded


def bundle_kernel(w_q, w_o, out):
    out[0] = w_q[...]
    for k in range(4):
        out[1, k * 128 : (k + 1) * 128, :] = w_o[:, k * 128 : (k + 1) * 128]


def query_kernel(x, wa, wb, cos, sin, out, w):
    w[:, :128], w[:, 128:] = wa[:2048], wb[:2048]
    both = jnp.dot(x[:, :2048], w[...], preferred_element_type=F32)
    for slot in range(RING):
        part = both[slot * 128 : (slot + 1) * 128]
        for pair in range(2):
            u = rope(part[:, pair * 128 : (pair + 1) * 128], cos[slot], sin[slot])
            out[slot, :, pair * 128 : (pair + 1) * 128] = (u * 0.125).astype(BF16)


def attend_kernel(place, q, kv, kv_c, before, before_c, *refs):
    out, keys, vals, scores, q4 = refs[-5:]
    step = pl.program_id(0)
    h, c = place[1], place[2]
    lanes = lax.broadcasted_iota(jnp.int32, (128, 128), 1)

    def place_block(src, k, half, core):
        both = src[k].astype(F32)
        turned = pltpu.roll(both, 64, 1)
        at = pl.ds(pl.multiple_of(half * 1024 + k * 256 + core * 128, 128), 128)
        keys[:, at] = jnp.where(lanes < 64, both, turned).T.astype(BF16)
        vals[at, :] = jnp.where(lanes < 64, turned, 1.0).astype(BF16)

    @pl.when(step == 0)
    def _():
        for k in range(RING):
            place_block(kv, k, h, c)
            place_block(kv_c, k, h, 1 - c)

    @pl.when((step == 0) & (h == 1))
    def _():
        for k in range(RING):
            place_block(before, k, 0, c)
            place_block(before_c, k, 0, 1 - c)

    for pair in range(2):
        block = q[0, :, pair * 128 : (pair + 1) * 128].astype(F32)
        q4[pair * 256 : pair * 256 + 128] = jnp.where(lanes < 64, block, 0.0).astype(BF16)
        q4[pair * 256 + 128 : pair * 256 + 256] = jnp.where(lanes < 64, 0.0, block).astype(BF16)
    last = h * (1024 // CHUNK) + step * 256 // CHUNK

    def dots(j):
        chunk = keys[:, pl.ds(pl.multiple_of(j * CHUNK, CHUNK), CHUNK)]
        return jnp.dot(q4[...], chunk, preferred_element_type=F32)

    def greatest(s):
        top = s[:, :128]
        for k in range(1, CHUNK // 128):
            top = jnp.maximum(top, s[:, k * 128 : (k + 1) * 128])
        return top

    s = dots(last)
    row = lax.rem(lax.broadcasted_iota(jnp.int32, s.shape, 0), 128) + c * 128 + lax.rem(step * 256, CHUNK)
    col = lax.broadcasted_iota(jnp.int32, s.shape, 1)
    s = jnp.where(col <= row, s, -1e30)
    scores[last] = s

    def first_pass(j, top):
        s = dots(j)
        scores[j] = s
        return jnp.maximum(top, greatest(s))

    top = lax.fori_loop(0, last, first_pass, greatest(s))
    top = jnp.max(top, axis=1, keepdims=True)

    def second_pass(j, acc):
        p = jnp.exp(scores[j] - top).astype(BF16)
        chunk = vals[pl.ds(pl.multiple_of(j * CHUNK, CHUNK), CHUNK), :]
        return acc + jnp.dot(p, chunk, preferred_element_type=F32)

    acc = lax.fori_loop(0, last + 1, second_pass, jnp.zeros((512, 128), F32))
    result = acc / pltpu.roll(acc, 64, 1)
    for pair in range(2):
        left = result[pair * 256 : pair * 256 + 128]
        right = pltpu.roll(result[pair * 256 + 128 : pair * 256 + 256], 64, 1)
        out[0, :, pair * 128 : (pair + 1) * 128] = jnp.where(lanes < 64, left, right).astype(BF16)


def gather_heads_kernel(place, parts, out):
    lanes = lax.broadcasted_iota(jnp.int32, (128, 128), 1)
    keep = jnp.where(place[3] == 0, 1.0, 0.0)
    for k in range(0, RING, 2):
        left, right = parts[k].astype(F32) * keep, parts[k + 1].astype(F32) * keep
        at = k // 2 * 128
        out[:, at : at + 128] = jnp.where(lanes < 64, left, pltpu.roll(right, 64, 1)).astype(BF16)
        out[:, 256 + at : 384 + at] = jnp.where(lanes < 64, pltpu.roll(left, 64, 1), right).astype(BF16)


def times_rows(att, wa, wb, w):
    for half, pieces in enumerate((wa, wb)):
        at = 0
        for piece, begin in pieces:
            for row in range(begin, piece.shape[0], 128):
                w[half * 128 : half * 128 + 128, at : at + 128] = piece[row : row + 128, :]
                at += 128
    return jnp.dot(att.reshape(256, 256), w[...], preferred_element_type=F32)


def out_own_kernel(near, far, qo, qo_c, z1, z1c, z2, z2c, total, w):
    total[...] = times_rows(near[0:2], [(qo, 2048)], [(qo_c, 2048)], w)
    total[...] += times_rows(far[0:2], [(z1, 2048), (z2, 0)], [(z1c, 2048), (z2c, 0)], w)


def out_beside_kernel(place, acts, base, near, far, o_b, o_bc, o_zb, o_zbc, fresh, mine, theirs, w):
    odd = lax.rem(place[0], 2)
    total = base[...] + times_rows(near[...], [(o_b, 0)], [(o_bc, 0)], w)
    total += times_rows(far[...], [(o_zb, 0)], [(o_zbc, 0)], w)
    low, high = total[:128], total[128:]
    mine[...] = (acts[...].astype(F32) + jnp.where(odd == 0, low, high)).astype(BF16)
    theirs[...] = jnp.where(odd == 0, high, low).astype(BF16)


def params(mib):
    return pltpu.CompilerParams(vmem_limit_bytes=mib * 2**20)


VM = pl.BlockSpec(memory_space=pltpu.VMEM)
SM = pl.BlockSpec(memory_space=pltpu.SMEM)


def prepare(acts, gain, first):
    return pl.pallas_call(
        prepare_kernel,
        out_shape=jax.ShapeDtypeStruct((RING, acts.shape[0], 2048 + 128), BF16),
        grid=(4,),
        in_specs=[
            pl.BlockSpec((32, 2048), lambda i: (i, 0)),
            pl.BlockSpec((1, 2048), lambda i: (0, 0)),
            pl.BlockSpec((32, 512), lambda i: (i, 0)),
        ],
        out_specs=pl.BlockSpec((RING, 32, 2048 + 128), lambda i: (0, i, 0)),
        compiler_params=params(16),
        cost_estimate=pl.CostEstimate(flops=2 * 512 * 2048 * 256, bytes_accessed=4 << 20, transcendentals=0),
    )(acts, gain, first)


def keyval(operands, *others):
    return pl.pallas_call(
        keyval_kernel,
        out_shape=(jax.ShapeDtypeStruct((4, 128, 256), BF16), jax.ShapeDtypeStruct((4, 128, 128), BF16)),
        in_specs=[SM] + [VM] * 6 + [pl.BlockSpec(memory_space=pl.ANY)] * len(others),
        out_specs=(VM, VM),
        scratch_shapes=[pltpu.VMEM((256, 2048), BF16)],
        compiler_params=params(24),
        cost_estimate=pl.CostEstimate(flops=2 * 512 * 2048 * 256, bytes_accessed=4 << 20, transcendentals=0),
    )(*operands, *others)


def query(x, wa, wb, cos, sin):
    return pl.pallas_call(
        query_kernel,
        out_shape=jax.ShapeDtypeStruct((4, 128, 256), BF16),
        in_specs=[VM] * 5,
        out_specs=VM,
        scratch_shapes=[pltpu.VMEM((2048, 256), BF16)],
        compiler_params=params(24),
        cost_estimate=pl.CostEstimate(flops=2 * 512 * 2048 * 256, bytes_accessed=4 << 20, transcendentals=0),
    )(x, wa, wb, cos, sin)


def attend(place, q, kvs, *others):
    def at(step, place):
        return (step, 0, 0)

    def to(step, place):
        return (lax.rem(step + place[0] // 2 * 2, RING), 0, 0)

    return pl.pallas_call(
        attend_kernel,
        out_shape=jax.ShapeDtypeStruct((4, 128, 256), BF16),
        grid_spec=pltpu.PrefetchScalarGridSpec(
            num_scalar_prefetch=1,
            grid=(RING,),
            in_specs=[
                pl.BlockSpec((1, 128, 256), at),
            ]
            + [pl.BlockSpec((RING, 128, 128), lambda step, place: (0, 0, place[4]))] * 4
            + [pl.BlockSpec(memory_space=pl.ANY)] * len(others),
            out_specs=pl.BlockSpec((1, 128, 256), to),
            scratch_shapes=[
                pltpu.VMEM((128, 2048), BF16),
                pltpu.VMEM((2048, 128), BF16),
                pltpu.VMEM((2048 // CHUNK, 512, CHUNK), F32),
                pltpu.VMEM((512, 128), BF16),
            ],
        ),
        compiler_params=params(24),
        cost_estimate=pl.CostEstimate(flops=2 * 2 * 512 * 256 * 6656, bytes_accessed=32 << 20, transcendentals=512 * 6656),
    )(place, q, *kvs, *others)


def bundle(w_q, w_o):
    return pl.pallas_call(
        bundle_kernel,
        out_shape=jax.ShapeDtypeStruct((2, 2048, 128), BF16),
        grid=(4,),
        in_specs=[pl.BlockSpec((512, 128), lambda i: (i, 0)), pl.BlockSpec((128, 512), lambda i: (0, i))],
        out_specs=pl.BlockSpec((2, 512, 128), lambda i: (0, i, 0)),
        compiler_params=params(16),
        cost_estimate=pl.CostEstimate(flops=0, bytes_accessed=2 << 20, transcendentals=0),
    )(w_q, w_o)


def out_own(*operands):
    return pl.pallas_call(
        out_own_kernel,
        out_shape=jax.ShapeDtypeStruct((256, 2048), F32),
        in_specs=[VM] * 8,
        out_specs=VM,
        scratch_shapes=[pltpu.VMEM((256, 2048), BF16)],
        compiler_params=params(32),
        cost_estimate=pl.CostEstimate(flops=2 * 256 * 512 * 2048, bytes_accessed=4 << 20, transcendentals=0),
    )(*operands)


def out_beside(*operands):
    return pl.pallas_call(
        out_beside_kernel,
        out_shape=(jax.ShapeDtypeStruct((128, 2048), BF16),) * 2,
        in_specs=[SM] + [VM] * 8 + [pl.BlockSpec(memory_space=pl.ANY)],
        out_specs=(VM, VM),
        scratch_shapes=[pltpu.VMEM((256, 2048), BF16)],
        compiler_params=params(32),
        cost_estimate=pl.CostEstimate(flops=2 * 256 * 512 * 2048, bytes_accessed=4 << 20, transcendentals=0),
    )(*operands)


def hold(arrays, *others):
    n = len(arrays)
    return pl.pallas_call(
        lambda *refs: None,
        out_shape=[jax.ShapeDtypeStruct(x.shape, x.dtype) for x in arrays],
        in_specs=[pl.BlockSpec(memory_space=pl.ANY)] * (n + len(others)),
        out_specs=[pl.BlockSpec(memory_space=pl.ANY)] * n,
        input_output_aliases={k: k for k in range(n)},
    )(*arrays, *others)


def gather_heads(place, parts):
    return pl.pallas_call(
        gather_heads_kernel,
        out_shape=jax.ShapeDtypeStruct((128, 512), BF16),
        in_specs=[SM, VM],
        out_specs=VM,
        cost_estimate=pl.CostEstimate(flops=0, bytes_accessed=1 << 18, transcendentals=0),
    )(place, parts)


def beside_b(x):
    return lax.ppermute(x, "y", [(y, RING - 1 - y) for y in range(RING)])


def swap(x):
    return lax.all_to_all(x, "y", 0, 0)


def per_device(acts, norm_gain, query_weight, kv_weight, out_weight, first_values, mix_weight):
    inputs = acts[0]
    tok = inputs.shape[0]
    h, y, c = lax.axis_index("zh"), lax.axis_index("y"), lax.axis_index("c")
    section = lax.axis_index("x") * ZS + lax.axis_index("zl")
    place = jnp.stack([y, h, c, section, h]).astype(jnp.int32)
    place_far = jnp.stack([y, h, c, section, 1 - h]).astype(jnp.int32)
    core = functools.partial(pull, axis="c", by=1)
    half = functools.partial(pull, axis="zh", by=1)

    positions = h * 8 * tok + (2 * jnp.arange(RING, dtype=jnp.int32)[:, None] + c) * tok + jnp.arange(tok, dtype=jnp.int32)
    cos, sin = (t.reshape(RING, tok, 128) for t in rope_tables(positions.reshape(-1), 64))
    mix_two = lax.dynamic_index_in_dim(mix_weight[0].reshape(2, RING), y, 1, keepdims=False)
    mix = jnp.broadcast_to(jnp.repeat(mix_two, 64)[None, :], (8, 128))

    x = swap(prepare(inputs, norm_gain, first_values[0]))

    w_kv = kv_weight[0].T
    home = [(s, s // 8 * 8 + s % 4 * 2 + s % 8 // 4) for s in range(16)]
    kv_b = lax.ppermute(w_kv, SEQ, [(s, (d + 8) % 16) for s, d in home])
    kv_a = lax.ppermute(w_kv, SEQ, home)
    mine = jnp.concatenate([kv_a, kv_b], axis=0)
    theirs = core(mine)

    qo = bundle(query_weight[0], out_weight[0])
    qo = qo.reshape(4096, 128)
    z1, qo_c = half(qo[:3072]), core(qo)
    x = x.reshape(RING * tok, 2048 + 128)
    kv, values = keyval((place, x, mine, theirs, cos, sin, mix))

    kv_c = core(kv)
    kv_before = lax.ppermute(kv, "zh", [(0, 1)])
    q_near = query(x, qo, qo_c, cos, sin)
    fresh = gather_heads(place, swap(values))
    kv_before, o_2 = hold([kv_before, qo[3072:]], q_near, fresh)
    kv_before_c = core(kv_before)
    kvs = (kv, kv_c, kv_before, kv_before_c)

    kv_before, o_2 = hold([kv_before, qo[3072:]], q_near, fresh)
    kv_before_c = core(kv_before)
    kvs = (kv, kv_c, kv_before, kv_before_c)

    def sent_on(x, stride):
        return [lax.ppermute(x, PIPE, [(p, p + k * stride) for p in range(stride)]) for k in range(1, 4)]

    def sent_on(x, *rounds):
        return sum([lax.ppermute(x, PIPE, pairs) for pairs in rounds], x)

    z1, o_own, fresh = hold([z1, qo[2048:], fresh], kv_before_c)
    fresh = sent_on(fresh, [(0, 2)])
    z2 = half(o_2)
    o_b = beside_b(o_own)
    att_near = attend(place, q_near, kvs)
    z1c = core(z1)
    q_far = query(x, z1, z1c, cos, sin)

    q_far, z2, o_b, fresh = hold([q_far, z2, o_b, fresh], att_near)
    fresh = sent_on(fresh, [(0, 1), (2, 3)])
    att_far = attend(place_far, q_far, kvs)
    o_zb = beside_b(jnp.concatenate([z1[2048:], z2], axis=0))
    near = beside_b(att_near[2:4])
    z2c, o_bc = core(z2), core(o_b)

    o_zb, fresh = hold([o_zb, fresh], att_far, near, z2c, o_bc)
    far = beside_b(att_far[2:4])
    o_zbc = core(o_zb)
    fresh = sent_on(fresh, *[[(p, p + k * ZS) for p in range(ZS)] for k in range(1, XS)])
    total = out_own(att_near, att_far, qo, qo_c, z1, z1c, z2, z2c)
    mine, theirs = out_beside(place, inputs, total, near, far, o_b, o_bc, o_zb, o_zbc, fresh)

    onward = [(p, (p + 1) % (XS * ZS)) for p in range(XS * ZS)]
    across = [(y * XS * ZS + p, (y ^ 1) * XS * ZS + q) for p, q in onward for y in range(RING)]
    sums = [lax.ppermute(theirs, ("y",) + PIPE, across), lax.ppermute(mine, PIPE, onward)]
    passed = (sums[0].astype(F32) + sums[1].astype(F32)).astype(BF16)
    return (passed[None], fresh[None])


def solution(mesh):
    split = Mesh(mesh.devices.reshape(HALVES, RING, CORES, XS, ZS), SEQ + PIPE)
    placed = (
        P(PIPE, SEQ, None),
        P(PIPE, None),
        P(PIPE, None, SEQ),
        P(PIPE, None, SEQ),
        P(PIPE, SEQ, None),
        P(PIPE, SEQ, None),
        P(PIPE, None),
    )
    return jax.shard_map(
        per_device,
        mesh=split,
        in_specs=placed,
        out_specs=(P(PIPE, SEQ, None), P(PIPE, SEQ, None)),
        check_vma=False,
    )
```

profile of v0, /device:TPU:136, one launch (start us, length us, event | category | flops | bytes accessed | tf_op | source)
XLA Modules:
  0.0 174.3 jit_solution(8305488264812258963)
XLA Ops:
  4.1 1.3 copy-done
  5.5 4.9 %all-to-all-start = ((bf16[4,128,2176]{2,1,0:T(8,128)(2,1)}), bf16[4,128,2176]{2,1,0:T(8,128)(2,1)S(1)}, u32[]{:S(2)}, u32[]{:S(2)}) async-start(bf16[4,128,2176]{2,1,0:T(8,128)(2,1)} %copy-done), calls=%async_computation | async-start | bytes 4456448 | tf_op jit(solution)/shard_map/all_to_all | solution.py:344
  10.4 3.4 %collective-permute-start.1 = (bf16[64,2048]{1,0:T(8,128)(2,1)}, bf16[64,2048]{1,0:T(8,128)(2,1)}, u32[]{:S(2)}, u32[]{:S(2)}) collective-permute-start(bf16[64,2048]{1,0:T(8,128)(2,1)} %bitcast.11), channel_id=1, source_target_pairs={{0,0},{16,32},{32,64},{48,96},{64,16},{80,48},{96,80},{112,112},{1... | collective-permute-start | bytes 786440 | tf_op jit(solution)/shard_map/ppermute | solution.py:367
  18.0 5.4 %collective-permute-start.7 = (bf16[3072,128]{1,0:T(8,128)(2,1)}, bf16[3072,128]{1,0:T(8,128)(2,1)}, u32[]{:S(2)}, u32[]{:S(2)}) collective-permute-start(bf16[3072,128]{1,0:T(8,128)(2,1)} %slice.30), channel_id=1, source_target_pairs={{128,0},{0,128},{129,1},{1,129},{130,2},{2,130},{131,3},{3,131},{1... | collective-permute-start | bytes 2359304 | tf_op jit(solution)/shard_map/ppermute | solution.py:39
  23.4 17.4 %collective-permute-done.1 = bf16[64,2048]{1,0:T(8,128)(2,1)} collective-permute-done((bf16[64,2048]{1,0:T(8,128)(2,1)}, bf16[64,2048]{1,0:T(8,128)(2,1)}, u32[]{:S(2)}, u32[]{:S(2)}) %collective-permute-start.1) | collective-permute-done | bytes 262176 | tf_op jit(solution)/shard_map/ppermute | solution.py:367
  40.8 1.7 constant_dynamic-update-slice_fusion.1
  43.2 1.1 collective-permute-start.3
  47.1 1.2 pad_maximum_fusion.1
  49.2 3.0 %shard_map.89 = (bf16[4,128,256]{2,1,0:T(8,128)(2,1)}, bf16[4,128,128]{2,1,0:T(8,128)(2,1)S(1)}) custom-call(s32[5]{0:T(128)S(1)} %stack.30.place, bf16[512,2176]{1,0:T(8,128)(2,1)S(1)} %bitcast.19, bf16[128,2048]{1,0:T(8,128)(2,1)} %constant_dynamic-update-slice_fusion.mine, bf16[128,2048]{1,0:T(8,128)(2,1)} %collective-permute-done.3.theirs, ...), custom_call_target="tpu_custom_call" | custom-call | flops 536870912 | bytes 4194304 | tf_op jit(solution)/shard_map/pallas_call | solution.py:228
  52.8 1.3 collective-permute-start.5
  54.1 6.0 %all-to-all-start.1 = ((bf16[4,128,128]{2,1,0:T(8,128)(2,1)}), bf16[4,128,128]{2,1,0:T(8,128)(2,1)}, u32[]{:S(2)}, u32[]{:S(2)}) async-start(bf16[4,128,128]{2,1,0:T(8,128)(2,1)} %copy-done.28), calls=%async_computation.1 | async-start | bytes 262144 | tf_op jit(solution)/shard_map/all_to_all | solution.py:344
  61.9 2.2 %shard_map.88.refs_2_.q = bf16[4,128,256]{2,1,0:T(8,128)(2,1)S(1)} custom-call(bf16[512,2176]{1,0:T(8,128)(2,1)S(1)} %bitcast.20, bf16[4096,128]{1,0:T(8,128)(2,1)S(1)} %bitcast.25, bf16[4096,128]{1,0:T(8,128)(2,1)} %collective-permute-done.wb.qo_c, f32[4,128,128]{2,1,0:T(8,128)S(1)} %get-tuple-element.37.cos, f32[4,128,128]{2,1,0:T(8,128)S(1)} %copy-done.2), custom_call_target="tpu_custom_call" | custom-call | flops 536870912 | bytes 4194304 | tf_op jit(solution)/shard_map/pallas_call | solution.py:240
  64.8 1.7 shard_map.90.refs_3_.refs_2_
  66.5 4.3 %collective-permute-done.5.refs_0_ = bf16[4,128,256]{2,1,0:T(8,128)(2,1)} collective-permute-done((bf16[4,128,256]{2,1,0:T(8,128)(2,1)}, bf16[4,128,256]{2,1,0:T(8,128)(2,1)}, u32[]{:S(2)}, u32[]{:S(2)}) %collective-permute-start.5) | collective-permute-done | bytes 262176 | tf_op jit(solution)/shard_map/ppermute | solution.py:378
  73.1 2.6 %collective-permute-start.10 = (bf16[2048,128]{1,0:T(8,128)(2,1)}, bf16[2048,128]{1,0:T(8,128)(2,1)}, u32[]{:S(2)}, u32[]{:S(2)}) collective-permute-start(bf16[2048,128]{1,0:T(8,128)(2,1)} %get-tuple-element.24), channel_id=1, source_target_pairs={{0,96},{32,64},{64,32},{96,0},{1,97},{33,65},{65,33},{97,1},{2,98}... | collective-permute-start | bytes 1572872 | tf_op jit(solution)/shard_map/ppermute | solution.py:340
  75.8 1.9 %collective-permute-start.9 = (bf16[1024,128]{1,0:T(8,128)(2,1)}, bf16[1024,128]{1,0:T(8,128)(2,1)S(1)}, u32[]{:S(2)}, u32[]{:S(2)}) collective-permute-start(bf16[1024,128]{1,0:T(8,128)(2,1)} %get-tuple-element.23), channel_id=1, source_target_pairs={{128,0},{0,128},{129,1},{1,129},{130,2},{2,130},{131,3},{3,131},{1... | collective-permute-start | bytes 786440 | tf_op jit(solution)/shard_map/ppermute | solution.py:39
  77.7 8.2 %collective-permute-start.11 = (bf16[128,512]{1,0:T(8,128)(2,1)}, bf16[128,512]{1,0:T(8,128)(2,1)S(1)}, u32[]{:S(2)}, u32[]{:S(2)}) collective-permute-start(bf16[128,512]{1,0:T(8,128)(2,1)} %get-tuple-element.25), channel_id=1, source_target_pairs={{0,2},{16,18},{32,34},{48,50},{64,66},{80,82},{96,98},{112,114},{1... | collective-permute-start | bytes 393224 | tf_op jit(solution)/shard_map/ppermute | solution.py:393
  86.9 12.6 %shard_map.93.refs_4_.near = bf16[4,128,256]{2,1,0:T(8,128)(2,1)S(1)} custom-call(s32[5]{0:T(128)S(1)} %copy-done.31, bf16[4,128,256]{2,1,0:T(8,128)(2,1)S(1)} %copy-done.7, bf16[4,128,256]{2,1,0:T(8,128)(2,1)} %get-tuple-element.18.kv, bf16[4,128,256]{2,1,0:T(8,128)(2,1)S(1)} %collective-permute-done.4.kv_c, bf16[4,128,256]{2,1,0:T(8,128)(2,1)} %get-tuple-element.21.before, ...), custom_call_target="tpu_custom_call" | custom-call | flops 3489660928 | bytes 33554432 | tf_op jit(solution)/shard_map/pallas_call | solution.py:258
  99.5 1.8 %slice.28 = bf16[1024,128]{1,0:T(8,128)(2,1)} slice(bf16[3072,128]{1,0:T(8,128)(2,1)} %get-tuple-element.22.wa.z1), slice={[2048:3072], [0:128]} | slice | bytes 524288 | tf_op jit(solution)/shard_map/slice | solution.py:406
  102.0 2.4 %shard_map.95.refs_0_ = bf16[4,128,256]{2,1,0:T(8,128)(2,1)S(1)} custom-call(bf16[512,2176]{1,0:T(8,128)(2,1)S(1)} %bitcast.21, bf16[3072,128]{1,0:T(8,128)(2,1)} %get-tuple-element.22.wa.z1, bf16[3072,128]{1,0:T(8,128)(2,1)S(1)} %collective-permute-done.8.wb.z1c, f32[4,128,128]{2,1,0:T(8,128)S(1)} %get-tuple-element.37.cos, f32[4,128,128]{2,1,0:T(8,128)S(1)} %copy-done.3), custom_call_target="tpu_custom_call" | custom-call | flops 536870912 | bytes 4194304 | tf_op jit(solution)/shard_map/pallas_call | solution.py:240
  105.9 1.9 %pad_maximum_fusion = bf16[2048,128]{1,0:T(8,128)(2,1)} fusion(bf16[1024,128]{1,0:T(8,128)(2,1)} %get-tuple-element.27.z2, bf16[1024,128]{1,0:T(8,128)(2,1)} %slice.28), kind=kLoop, calls=%fused_computation.3 | loop fusion | flops 1048576 | bytes 1048576 | tf_op jit(solution)/shard_map/concatenate | solution.py:406
  107.9 2.1 %collective-permute-start.13 = (bf16[2,128,256]{2,1,0:T(8,128)(2,1)S(1)}, bf16[2,128,256]{2,1,0:T(8,128)(2,1)S(1)}, u32[]{:S(2)}, u32[]{:S(2)}) collective-permute-start(bf16[2,128,256]{2,1,0:T(8,128)(2,1)S(1)} %slice.32), channel_id=1, source_target_pairs={{0,96},{32,64},{64,32},{96,0},{1,97},{33,65},{65,33},{97,1},{2,98}... | collective-permute-start | bytes 393224 | tf_op jit(solution)/shard_map/ppermute | solution.py:340
  110.2 1.3 collective-permute-start.17
  112.5 12.6 %shard_map.97.far.refs_2_ = bf16[4,128,256]{2,1,0:T(8,128)(2,1)S(1)} custom-call(s32[5]{0:T(128)S(1)} %stack.32.place, bf16[4,128,256]{2,1,0:T(8,128)(2,1)S(1)} %copy-done.19, bf16[4,128,256]{2,1,0:T(8,128)(2,1)} %get-tuple-element.18.kv, bf16[4,128,256]{2,1,0:T(8,128)(2,1)S(1)} %copy-done.33, bf16[4,128,256]{2,1,0:T(8,128)(2,1)} %get-tuple-element.21.before, ...), custom_call_target="tpu_custom_call" | custom-call | flops 3489660928 | bytes 33554432 | tf_op jit(solution)/shard_map/pallas_call | solution.py:258
  127.6 1.9 %collective-permute-start.19 = (bf16[128,512]{1,0:T(8,128)(2,1)}, bf16[128,512]{1,0:T(8,128)(2,1)S(1)}, u32[]{:S(2)}, u32[]{:S(2)}) collective-permute-start(bf16[128,512]{1,0:T(8,128)(2,1)} %get-tuple-element.31), channel_id=1, source_target_pairs={{0,4},{1,5},{2,6},{3,7},{16,20},{17,21},{18,22},{19,23},{32,36},{3... | collective-permute-start | bytes 393224 | tf_op jit(solution)/shard_map/ppermute | solution.py:393
  129.5 2.2 %collective-permute-start.20 = (bf16[128,512]{1,0:T(8,128)(2,1)}, bf16[128,512]{1,0:T(8,128)(2,1)S(1)}, u32[]{:S(2)}, u32[]{:S(2)}) collective-permute-start(bf16[128,512]{1,0:T(8,128)(2,1)} %get-tuple-element.31), channel_id=1, source_target_pairs={{0,8},{1,9},{2,10},{3,11},{16,24},{17,25},{18,26},{19,27},{32,40},... | collective-permute-start | bytes 393224 | tf_op jit(solution)/shard_map/ppermute | solution.py:393
  131.7 1.3 collective-permute-start.21
  136.5 2.5 %shard_map.98.base = f32[256,2048]{1,0:T(8,128)S(1)} custom-call(bf16[4,128,256]{2,1,0:T(8,128)(2,1)S(1)} %copy-done.17, bf16[4,128,256]{2,1,0:T(8,128)(2,1)S(1)} %copy-done.15, bf16[4096,128]{1,0:T(8,128)(2,1)S(1)} %bitcast.26, bf16[4096,128]{1,0:T(8,128)(2,1)} %collective-permute-done.wb.qo_c, bf16[3072,128]{1,0:T(8,128)(2,1)} %get-tuple-element.22.wa.z1, ...), custom_call_target="tpu_custom_call" | custom-call | flops 536870912 | bytes 4194304 | tf_op jit(solution)/shard_map/pallas_call | solution.py:295
  139.4 2.2 %shard_map.100 = (bf16[128,2048]{1,0:T(8,128)(2,1)S(1)}, bf16[128,2048]{1,0:T(8,128)(2,1)S(1)}) custom-call(s32[5]{0:T(128)S(1)} %copy-done.31, bf16[128,2048]{1,0:T(8,128)(2,1)S(1)} %bitcast.28, f32[256,2048]{1,0:T(8,128)S(1)} %shard_map.98.base, bf16[2,128,256]{2,1,0:T(8,128)(2,1)S(1)} %copy-done.25, bf16[2,128,256]{2,1,0:T(8,128)(2,1)S(1)} %collective-permute-done.14.far, ...), custom_call_target="tpu_custom_call" | custom-call | flops 536870912 | bytes 4194304 | tf_op jit(solution)/shard_map/pallas_call | solution.py:307
  141.9 2.1 %collective-permute-start.23 = (bf16[128,2048]{1,0:T(8,128)(2,1)S(1)}, bf16[128,2048]{1,0:T(8,128)(2,1)S(1)}, u32[]{:S(2)}, u32[]{:S(2)}) collective-permute-start(bf16[128,2048]{1,0:T(8,128)(2,1)S(1)} %get-tuple-element.33), channel_id=1, source_target_pairs={{0,1},{1,2},{2,3},{3,4},{4,5},{5,6},{6,7},{7,8},{8,9},{9,10},{10,1... | collective-permute-start | bytes 1572872 | tf_op jit(solution)/shard_map/ppermute | solution.py:419
  144.0 17.4 %collective-permute-done.22 = bf16[128,2048]{1,0:T(8,128)(2,1)S(1)} collective-permute-done((bf16[128,2048]{1,0:T(8,128)(2,1)S(1)}, bf16[128,2048]{1,0:T(8,128)(2,1)S(1)}, u32[]{:S(2)}, u32[]{:S(2)}) %collective-permute-start.22) | collective-permute-done | bytes 524320 | tf_op jit(solution)/shard_map/ppermute | solution.py:419
  161.4 12.0 %collective-permute-done.23 = bf16[128,2048]{1,0:T(8,128)(2,1)S(1)} collective-permute-done((bf16[128,2048]{1,0:T(8,128)(2,1)S(1)}, bf16[128,2048]{1,0:T(8,128)(2,1)S(1)}, u32[]{:S(2)}, u32[]{:S(2)}) %collective-permute-start.23) | collective-permute-done | bytes 524320 | tf_op jit(solution)/shard_map/ppermute | solution.py:419
  (141 shorter events, 29.6 us)
Async XLA Ops:
  5.5 42.8 %all-to-all-start = ((bf16[4,128,2176]{2,1,0:T(8,128)(2,1)}), bf16[4,128,2176]{2,1,0:T(8,128)(2,1)S(1)}, u32[]{:S(2)}, u32[]{:S(2)}) async-start(bf16[4,128,2176]{2,1,0:T(8,128)(2,1)} %copy-done), calls=%async_computation | async-start | bytes 4456448 | tf_op jit(solution)/shard_map/all_to_all | solution.py:344
  10.4 30.4 %collective-permute-start.1 = (bf16[64,2048]{1,0:T(8,128)(2,1)}, bf16[64,2048]{1,0:T(8,128)(2,1)}, u32[]{:S(2)}, u32[]{:S(2)}) collective-permute-start(bf16[64,2048]{1,0:T(8,128)(2,1)} %bitcast.11), channel_id=1, source_target_pairs={{0,0},{16,32},{32,64},{48,96},{64,16},{80,48},{96,80},{112,112},{1... | collective-permute-start | bytes 786440 | tf_op jit(solution)/shard_map/ppermute | solution.py:367
  13.7 28.7 %collective-permute-start.2 = (bf16[64,2048]{1,0:T(8,128)(2,1)}, bf16[64,2048]{1,0:T(8,128)(2,1)S(1)}, u32[]{:S(2)}, u32[]{:S(2)}) collective-permute-start(bf16[64,2048]{1,0:T(8,128)(2,1)} %bitcast.11), channel_id=1, source_target_pairs={{0,128},{16,160},{32,192},{48,224},{64,144},{80,176},{96,208},{112... | collective-permute-start | bytes 786440 | tf_op jit(solution)/shard_map/ppermute | solution.py:366
  15.9 28.9 %copy-start.38 = (f32[1,8]{1,0:T(1,128)S(1)}, f32[1,8]{1,0:T(1,128)}, u32[]{:S(2)}) copy-start(f32[1,8]{1,0:T(1,128)} %param.13) | copy-start | bytes 100
  16.3 44.7 %collective-permute-start = (bf16[4096,128]{1,0:T(8,128)(2,1)S(1)}, bf16[4096,128]{1,0:T(8,128)(2,1)}, u32[]{:S(2)}, u32[]{:S(2)}) collective-permute-start(bf16[4096,128]{1,0:T(8,128)(2,1)S(1)} %bitcast.22), channel_id=1, source_target_pairs={{16,0},{0,16},{17,1},{1,17},{18,2},{2,18},{19,3},{3,19},{20,4},{4,... | collective-permute-start | bytes 3145736 | tf_op jit(solution)/shard_map/ppermute | solution.py:39
  18.0 53.6 %collective-permute-start.7 = (bf16[3072,128]{1,0:T(8,128)(2,1)}, bf16[3072,128]{1,0:T(8,128)(2,1)}, u32[]{:S(2)}, u32[]{:S(2)}) collective-permute-start(bf16[3072,128]{1,0:T(8,128)(2,1)} %slice.30), channel_id=1, source_target_pairs={{128,0},{0,128},{129,1},{1,129},{130,2},{2,130},{131,3},{3,131},{1... | collective-permute-start | bytes 2359304 | tf_op jit(solution)/shard_map/ppermute | solution.py:39
  43.2 5.0 %collective-permute-start.3 = (bf16[128,2048]{1,0:T(8,128)(2,1)}, bf16[128,2048]{1,0:T(8,128)(2,1)}, u32[]{:S(2)}, u32[]{:S(2)}) collective-permute-start(bf16[128,2048]{1,0:T(8,128)(2,1)} %constant_dynamic-update-slice_fusion.mine), channel_id=1, source_target_pairs={{16,0},{0,16},{17,1},{1,17},{18,2},{2,18},{19,3},{3,19},{20,4},{4,... | collective-permute-start | bytes 1572872 | tf_op jit(solution)/shard_map/ppermute | solution.py:39
  52.8 17.9 %collective-permute-start.5 = (bf16[4,128,256]{2,1,0:T(8,128)(2,1)}, bf16[4,128,256]{2,1,0:T(8,128)(2,1)}, u32[]{:S(2)}, u32[]{:S(2)}) collective-permute-start(bf16[4,128,256]{2,1,0:T(8,128)(2,1)} %get-tuple-element.18.kv), channel_id=1, source_target_pairs={{0,128},{1,129},{2,130},{3,131},{4,132},{5,133},{6,134},{7,135},{8... | collective-permute-start | bytes 786440 | tf_op jit(solution)/shard_map/ppermute | solution.py:378
  54.1 10.7 %all-to-all-start.1 = ((bf16[4,128,128]{2,1,0:T(8,128)(2,1)}), bf16[4,128,128]{2,1,0:T(8,128)(2,1)}, u32[]{:S(2)}, u32[]{:S(2)}) async-start(bf16[4,128,128]{2,1,0:T(8,128)(2,1)} %copy-done.28), calls=%async_computation.1 | async-start | bytes 262144 | tf_op jit(solution)/shard_map/all_to_all | solution.py:344
  66.5 19.4 %copy-start.31 = (s32[5]{0:T(128)S(1)}, s32[5]{0:T(128)}, u32[]{:S(2)}) copy-start(s32[5]{0:T(128)} %copy-done.30) | copy-start | bytes 64
  70.8 1.9 %collective-permute-start.6 = (bf16[4,128,256]{2,1,0:T(8,128)(2,1)}, bf16[4,128,256]{2,1,0:T(8,128)(2,1)}, u32[]{:S(2)}, u32[]{:S(2)}) collective-permute-start(bf16[4,128,256]{2,1,0:T(8,128)(2,1)} %get-tuple-element.21.before), channel_id=1, source_target_pairs={{16,0},{0,16},{17,1},{1,17},{18,2},{2,18},{19,3},{3,19},{20,4},{4,... | collective-permute-start | bytes 786440 | tf_op jit(solution)/shard_map/ppermute | solution.py:39
  72.6 29.3 %collective-permute-start.8 = (bf16[3072,128]{1,0:T(8,128)(2,1)}, bf16[3072,128]{1,0:T(8,128)(2,1)S(1)}, u32[]{:S(2)}, u32[]{:S(2)}) collective-permute-start(bf16[3072,128]{1,0:T(8,128)(2,1)} %get-tuple-element.22.wa.z1), channel_id=1, source_target_pairs={{16,0},{0,16},{17,1},{1,17},{18,2},{2,18},{19,3},{3,19},{20,4},{4,... | collective-permute-start | bytes 2359304 | tf_op jit(solution)/shard_map/ppermute | solution.py:39
  72.8 13.2 %collective-permute-start.4 = (bf16[4,128,256]{2,1,0:T(8,128)(2,1)}, bf16[4,128,256]{2,1,0:T(8,128)(2,1)S(1)}, u32[]{:S(2)}, u32[]{:S(2)}) collective-permute-start(bf16[4,128,256]{2,1,0:T(8,128)(2,1)} %get-tuple-element.18.kv), channel_id=1, source_target_pairs={{16,0},{0,16},{17,1},{1,17},{18,2},{2,18},{19,3},{3,19},{20,4},{4,... | collective-permute-start | bytes 786440 | tf_op jit(solution)/shard_map/ppermute | solution.py:39
  73.1 32.7 %collective-permute-start.10 = (bf16[2048,128]{1,0:T(8,128)(2,1)}, bf16[2048,128]{1,0:T(8,128)(2,1)}, u32[]{:S(2)}, u32[]{:S(2)}) collective-permute-start(bf16[2048,128]{1,0:T(8,128)(2,1)} %get-tuple-element.24), channel_id=1, source_target_pairs={{0,96},{32,64},{64,32},{96,0},{1,97},{33,65},{65,33},{97,1},{2,98}... | collective-permute-start | bytes 1572872 | tf_op jit(solution)/shard_map/ppermute | solution.py:340
  75.8 29.3 %collective-permute-start.9 = (bf16[1024,128]{1,0:T(8,128)(2,1)}, bf16[1024,128]{1,0:T(8,128)(2,1)S(1)}, u32[]{:S(2)}, u32[]{:S(2)}) collective-permute-start(bf16[1024,128]{1,0:T(8,128)(2,1)} %get-tuple-element.23), channel_id=1, source_target_pairs={{128,0},{0,128},{129,1},{1,129},{130,2},{2,130},{131,3},{3,131},{1... | collective-permute-start | bytes 786440 | tf_op jit(solution)/shard_map/ppermute | solution.py:39
  77.7 24.3 %copy-start.3 = (f32[4,128,128]{2,1,0:T(8,128)S(1)}, f32[4,128,128]{2,1,0:T(8,128)}, u32[]{:S(2)}) copy-start(f32[4,128,128]{2,1,0:T(8,128)} %get-tuple-element.38.sin) | copy-start | bytes 786436
  77.7 23.6 %collective-permute-start.11 = (bf16[128,512]{1,0:T(8,128)(2,1)}, bf16[128,512]{1,0:T(8,128)(2,1)S(1)}, u32[]{:S(2)}, u32[]{:S(2)}) collective-permute-start(bf16[128,512]{1,0:T(8,128)(2,1)} %get-tuple-element.25), channel_id=1, source_target_pairs={{0,2},{16,18},{32,34},{48,50},{64,66},{80,82},{96,98},{112,114},{1... | collective-permute-start | bytes 393224 | tf_op jit(solution)/shard_map/ppermute | solution.py:393
  86.9 12.6 %copy-start.32 = (bf16[4,128,256]{2,1,0:T(8,128)(2,1)}, bf16[4,128,256]{2,1,0:T(8,128)(2,1)S(1)}, u32[]{:S(2)}) copy-start(bf16[4,128,256]{2,1,0:T(8,128)(2,1)S(1)} %collective-permute-done.4.kv_c) | copy-start | bytes 786436
  86.9 14.4 %copy-start.34 = (bf16[128,512]{1,0:T(8,128)(2,1)S(1)}, bf16[128,512]{1,0:T(8,128)(2,1)}, u32[]{:S(2)}) copy-start(bf16[128,512]{1,0:T(8,128)(2,1)} %get-tuple-element.25) | copy-start | bytes 393220
  107.8 18.8 %collective-permute-start.16 = (bf16[2048,128]{1,0:T(8,128)(2,1)}, bf16[2048,128]{1,0:T(8,128)(2,1)}, u32[]{:S(2)}, u32[]{:S(2)}) collective-permute-start(bf16[2048,128]{1,0:T(8,128)(2,1)} %pad_maximum_fusion), channel_id=1, source_target_pairs={{0,96},{32,64},{64,32},{96,0},{1,97},{33,65},{65,33},{97,1},{2,98}... | collective-permute-start | bytes 1572872 | tf_op jit(solution)/shard_map/ppermute | solution.py:340
  107.8 18.8 %collective-permute-start.15 = (bf16[2048,128]{1,0:T(8,128)(2,1)}, bf16[2048,128]{1,0:T(8,128)(2,1)S(1)}, u32[]{:S(2)}, u32[]{:S(2)}) collective-permute-start(bf16[2048,128]{1,0:T(8,128)(2,1)} %get-tuple-element.28.o_b), channel_id=1, source_target_pairs={{16,0},{0,16},{17,1},{1,17},{18,2},{2,18},{19,3},{3,19},{20,4},{4,... | collective-permute-start | bytes 1572872 | tf_op jit(solution)/shard_map/ppermute | solution.py:39
  107.9 17.9 %collective-permute-start.13 = (bf16[2,128,256]{2,1,0:T(8,128)(2,1)S(1)}, bf16[2,128,256]{2,1,0:T(8,128)(2,1)S(1)}, u32[]{:S(2)}, u32[]{:S(2)}) collective-permute-start(bf16[2,128,256]{2,1,0:T(8,128)(2,1)S(1)} %slice.32), channel_id=1, source_target_pairs={{0,96},{32,64},{64,32},{96,0},{1,97},{33,65},{65,33},{97,1},{2,98}... | collective-permute-start | bytes 393224 | tf_op jit(solution)/shard_map/ppermute | solution.py:340
  110.0 15.8 %collective-permute-start.12 = (bf16[1024,128]{1,0:T(8,128)(2,1)}, bf16[1024,128]{1,0:T(8,128)(2,1)S(1)}, u32[]{:S(2)}, u32[]{:S(2)}) collective-permute-start(bf16[1024,128]{1,0:T(8,128)(2,1)} %get-tuple-element.27.z2), channel_id=1, source_target_pairs={{16,0},{0,16},{17,1},{1,17},{18,2},{2,18},{19,3},{3,19},{20,4},{4,... | collective-permute-start | bytes 786440 | tf_op jit(solution)/shard_map/ppermute | solution.py:39
  110.2 14.9 %collective-permute-start.17 = (bf16[128,512]{1,0:T(8,128)(2,1)}, bf16[128,512]{1,0:T(8,128)(2,1)S(1)}, u32[]{:S(2)}, u32[]{:S(2)}) collective-permute-start(bf16[128,512]{1,0:T(8,128)(2,1)} %get-tuple-element.29), channel_id=1, source_target_pairs={{0,1},{2,3},{16,17},{18,19},{32,33},{34,35},{48,49},{50,51},{64,65... | collective-permute-start | bytes 393224 | tf_op jit(solution)/shard_map/ppermute | solution.py:393
  112.5 12.6 %copy-start.37 = (bf16[128,512]{1,0:T(8,128)(2,1)S(1)}, bf16[128,512]{1,0:T(8,128)(2,1)}, u32[]{:S(2)}) copy-start(bf16[128,512]{1,0:T(8,128)(2,1)} %get-tuple-element.29) | copy-start | bytes 393220
  127.3 12.1 %collective-permute-start.18 = (bf16[2048,128]{1,0:T(8,128)(2,1)}, bf16[2048,128]{1,0:T(8,128)(2,1)S(1)}, u32[]{:S(2)}, u32[]{:S(2)}) collective-permute-start(bf16[2048,128]{1,0:T(8,128)(2,1)} %get-tuple-element.30.o_zb), channel_id=1, source_target_pairs={{16,0},{0,16},{17,1},{1,17},{18,2},{2,18},{19,3},{3,19},{20,4},{4,... | collective-permute-start | bytes 1572872 | tf_op jit(solution)/shard_map/ppermute | solution.py:39
  127.6 11.4 %collective-permute-start.19 = (bf16[128,512]{1,0:T(8,128)(2,1)}, bf16[128,512]{1,0:T(8,128)(2,1)S(1)}, u32[]{:S(2)}, u32[]{:S(2)}) collective-permute-start(bf16[128,512]{1,0:T(8,128)(2,1)} %get-tuple-element.31), channel_id=1, source_target_pairs={{0,4},{1,5},{2,6},{3,7},{16,20},{17,21},{18,22},{19,23},{32,36},{3... | collective-permute-start | bytes 393224 | tf_op jit(solution)/shard_map/ppermute | solution.py:393
  129.5 9.5 %collective-permute-start.20 = (bf16[128,512]{1,0:T(8,128)(2,1)}, bf16[128,512]{1,0:T(8,128)(2,1)S(1)}, u32[]{:S(2)}, u32[]{:S(2)}) collective-permute-start(bf16[128,512]{1,0:T(8,128)(2,1)} %get-tuple-element.31), channel_id=1, source_target_pairs={{0,8},{1,9},{2,10},{3,11},{16,24},{17,25},{18,26},{19,27},{32,40},... | collective-permute-start | bytes 393224 | tf_op jit(solution)/shard_map/ppermute | solution.py:393
  131.7 7.3 %collective-permute-start.21 = (bf16[128,512]{1,0:T(8,128)(2,1)}, bf16[128,512]{1,0:T(8,128)(2,1)S(1)}, u32[]{:S(2)}, u32[]{:S(2)}) collective-permute-start(bf16[128,512]{1,0:T(8,128)(2,1)} %get-tuple-element.31), channel_id=1, source_target_pairs={{0,12},{1,13},{2,14},{3,15},{16,28},{17,29},{18,30},{19,31},{32,44... | collective-permute-start | bytes 393224 | tf_op jit(solution)/shard_map/ppermute | solution.py:393
  133.9 5.4 %collective-permute-start.14 = (bf16[2,128,256]{2,1,0:T(8,128)(2,1)S(1)}, bf16[2,128,256]{2,1,0:T(8,128)(2,1)S(1)}, u32[]{:S(2)}, u32[]{:S(2)}) collective-permute-start(bf16[2,128,256]{2,1,0:T(8,128)(2,1)S(1)} %slice.33), channel_id=1, source_target_pairs={{0,96},{32,64},{64,32},{96,0},{1,97},{33,65},{65,33},{97,1},{2,98}... | collective-permute-start | bytes 393224 | tf_op jit(solution)/shard_map/ppermute | solution.py:340
  141.6 19.7 %collective-permute-start.22 = (bf16[128,2048]{1,0:T(8,128)(2,1)S(1)}, bf16[128,2048]{1,0:T(8,128)(2,1)S(1)}, u32[]{:S(2)}, u32[]{:S(2)}) collective-permute-start(bf16[128,2048]{1,0:T(8,128)(2,1)S(1)} %get-tuple-element.32), channel_id=1, source_target_pairs={{0,33},{32,1},{64,97},{96,65},{1,34},{33,2},{65,98},{97,66},{2,35}... | collective-permute-start | bytes 1572872 | tf_op jit(solution)/shard_map/ppermute | solution.py:419
  141.9 31.5 %collective-permute-start.23 = (bf16[128,2048]{1,0:T(8,128)(2,1)S(1)}, bf16[128,2048]{1,0:T(8,128)(2,1)S(1)}, u32[]{:S(2)}, u32[]{:S(2)}) collective-permute-start(bf16[128,2048]{1,0:T(8,128)(2,1)S(1)} %get-tuple-element.33), channel_id=1, source_target_pairs={{0,1},{1,2},{2,3},{3,4},{4,5},{5,6},{6,7},{7,8},{8,9},{9,10},{10,1... | collective-permute-start | bytes 1572872 | tf_op jit(solution)/shard_map/ppermute | solution.py:419
  (33 other events, 79.0 us)
where the time goes:
time: 176 us; the launch traced here: 174 us
  waiting for transfers between devices  52.4 us (30%)
  starting transfers between devices  48.5 us (28%)
  Pallas kernels  40.2 us (23%)
  local copies, waits for them, and re-layouts  24.9 us (14%)
  other arithmetic  7.15 us (4%)
    pallas_call x2, Pallas kernels, attend(): pl.pallas_call(attend_kernel, out_shape=jax.ShapeDtypeStruct((4, 128, 256...  25.1 us
    unnamed x81, local copies, waits for them, and re-layouts  19.1 us
    ppermute x1, waiting for transfers between devices, per_device(): kv_a = lax.ppermute(w_kv, SEQ, home)  17.4 us
    ppermute x1, waiting for transfers between devices, per_device(): lax.ppermute(theirs, ('y',) + PIPE, across)  17.4 us
    ppermute x5, starting transfers between devices, sent_on(): return sum([lax.ppermute(x, PIPE, pairs) for pairs in rounds], x)  14.9 us
    ppermute x1, waiting for transfers between devices, per_device(): lax.ppermute(mine, PIPE, onward)  12 us
    all_to_all x2, starting transfers between devices, swap(): return lax.all_to_all(x, 'y', 0, 0)  10.9 us
    ppermute x10, starting transfers between devices, pull(): return lax.ppermute(x, axis, [((i + by) % n, i) for i in range(n)])  10.2 us
  transfers between devices with their start and end apart: 26, of which 6 were waited for; matrix products, arithmetic and copies ran while one was open for 7% of the time, Pallas kernels for 21%

commit v1 on v0

--- a/solution.py
+++ b/solution.py
@@ -389,11 +389,13 @@
     def sent_on(x, stride):
         return [lax.ppermute(x, PIPE, [(p, p + k * stride) for p in range(stride)]) for k in range(1, 4)]
 
-    def sent_on(x, *rounds):
-        return sum([lax.ppermute(x, PIPE, pairs) for pairs in rounds], x)
+    def sent_on(x, by):
+        return x + lax.ppermute(x, PIPE, [(p, p + by) for p in range(0, XS * ZS, 2 * by)])
+
+    fresh = sent_on(fresh, 8)
 
     z1, o_own, fresh = hold([z1, qo[2048:], fresh], kv_before_c)
-    fresh = sent_on(fresh, [(0, 2)])
+    fresh = sent_on(fresh, 4)
     z2 = half(o_2)
     o_b = beside_b(o_own)
     att_near = attend(place, q_near, kvs)
@@ -401,7 +403,7 @@
     q_far = query(x, z1, z1c, cos, sin)
 
     q_far, z2, o_b, fresh = hold([q_far, z2, o_b, fresh], att_near)
-    fresh = sent_on(fresh, [(0, 1), (2, 3)])
+    fresh = sent_on(fresh, 2)
     att_far = attend(place_far, q_far, kvs)
     o_zb = beside_b(jnp.concatenate([z1[2048:], z2], axis=0))
     near = beside_b(att_near[2:4])
@@ -410,7 +412,7 @@
     o_zb, fresh = hold([o_zb, fresh], att_far, near, z2c, o_bc)
     far = beside_b(att_far[2:4])
     o_zbc = core(o_zb)
-    fresh = sent_on(fresh, *[[(p, p + k * ZS) for p in range(ZS)] for k in range(1, XS)])
+    fresh = sent_on(fresh, 1)
     total = out_own(att_near, att_far, qo, qo_c, z1, z1c, z2, z2c)
     mine, theirs = out_beside(place, inputs, total, near, far, o_b, o_bc, o_zb, o_zbc, fresh)
 

time: 176 us -> 180 us (1.023)
  starting transfers between devices: 48.5 us -> 53.5 us
  waiting for transfers between devices: 52.4 us -> 49.6 us
    ppermute x10, starting transfers between devices: 10.2 us -> 15.5 us  [pull(): return lax.ppermute(x, axis, [((i + by) % n, i) for i in range(n)])]
    ppermute x1, waiting for transfers between devices: 4.26 us -> 0.01 us  [per_device(): kv_before = lax.ppermute(kv, 'zh', [(0, 1)])]
    ppermute x1, starting transfers between devices: 2.11 us -> 0.01 us  [per_device(): lax.ppermute(mine, PIPE, onward)]
    ppermute x5 -> x4, starting transfers between devices: 14.9 us -> 16.1 us  [sent_on(): lax.ppermute(x, PIPE, [(p, p + by) for p in range(0, XS * ZS, 2 * by)])]
    unnamed x81 -> x87, local copies, waits for them, and re-layouts: 19.1 us -> 19.9 us
  transfers between devices with their start and end apart: 26 -> 25, of which waited for: 6 -> 5; matrix products, arithmetic and copies ran while one was open for 7% -> 8% of each run, Pallas kernels for 21% -> 21%
where the time goes in v1:
time: 180 us; the launch traced here: 179 us
  starting transfers between devices  53.5 us (30%)
  waiting for transfers between devices  49.6 us (28%)
  Pallas kernels  40.1 us (22%)
  local copies, waits for them, and re-layouts  25.8 us (14%)
  other arithmetic  8.81 us (5%)
    pallas_call x2, Pallas kernels, attend(): pl.pallas_call(attend_kernel, out_shape=jax.ShapeDtypeStruct((4, 128, 256...  25.1 us
    unnamed x87, local copies, waits for them, and re-layouts  19.9 us
    ppermute x1, waiting for transfers between devices, per_device(): lax.ppermute(theirs, ('y',) + PIPE, across)  17.7 us
    ppermute x1, waiting for transfers between devices, per_device(): kv_a = lax.ppermute(w_kv, SEQ, home)  17.4 us
    ppermute x4, starting transfers between devices, sent_on(): lax.ppermute(x, PIPE, [(p, p + by) for p in range(0, XS * ZS, 2 * by)])  16.1 us
    ppermute x10, starting transfers between devices, pull(): return lax.ppermute(x, axis, [((i + by) % n, i) for i in range(n)])  15.5 us
    ppermute x1, waiting for transfers between devices, per_device(): lax.ppermute(mine, PIPE, onward)  12.3 us
    all_to_all x2, starting transfers between devices, swap(): return lax.all_to_all(x, 'y', 0, 0)  10.9 us
  transfers between devices with their start and end apart: 25, of which 5 were waited for; matrix products, arithmetic and copies ran while one was open for 8% of the time, Pallas kernels for 21%

profile of v1, /device:TPU:136, one launch (start us, length us, event | category | flops | bytes accessed | tf_op | source)
XLA Modules:
  0.0 178.8 jit_solution(12927496469261127753)
XLA Ops:
  4.1 1.4 copy-done
  5.5 4.9 %all-to-all-start = ((bf16[4,128,2176]{2,1,0:T(8,128)(2,1)}), bf16[4,128,2176]{2,1,0:T(8,128)(2,1)S(1)}, u32[]{:S(2)}, u32[]{:S(2)}) async-start(bf16[4,128,2176]{2,1,0:T(8,128)(2,1)} %copy-done), calls=%async_computation | async-start | bytes 4456448 | tf_op jit(solution)/shard_map/all_to_all | solution.py:344
  10.4 3.4 %collective-permute-start.1 = (bf16[64,2048]{1,0:T(8,128)(2,1)}, bf16[64,2048]{1,0:T(8,128)(2,1)}, u32[]{:S(2)}, u32[]{:S(2)}) collective-permute-start(bf16[64,2048]{1,0:T(8,128)(2,1)} %bitcast.11), channel_id=1, source_target_pairs={{0,0},{16,32},{32,64},{48,96},{64,16},{80,48},{96,80},{112,112},{1... | collective-permute-start | bytes 786440 | tf_op jit(solution)/shard_map/ppermute | solution.py:367
  18.0 5.4 %collective-permute-start.7 = (bf16[3072,128]{1,0:T(8,128)(2,1)}, bf16[3072,128]{1,0:T(8,128)(2,1)}, u32[]{:S(2)}, u32[]{:S(2)}) collective-permute-start(bf16[3072,128]{1,0:T(8,128)(2,1)} %slice.30), channel_id=1, source_target_pairs={{128,0},{0,128},{129,1},{1,129},{130,2},{2,130},{131,3},{3,131},{1... | collective-permute-start | bytes 2359304 | tf_op jit(solution)/shard_map/ppermute | solution.py:39
  23.4 17.4 %collective-permute-done.1 = bf16[64,2048]{1,0:T(8,128)(2,1)} collective-permute-done((bf16[64,2048]{1,0:T(8,128)(2,1)}, bf16[64,2048]{1,0:T(8,128)(2,1)}, u32[]{:S(2)}, u32[]{:S(2)}) %collective-permute-start.1) | collective-permute-done | bytes 262176 | tf_op jit(solution)/shard_map/ppermute | solution.py:367
  40.8 1.7 constant_dynamic-update-slice_fusion.1
  43.2 1.1 collective-permute-start.3
  47.1 1.2 pad_maximum_fusion.1
  49.2 3.0 %shard_map.89 = (bf16[4,128,256]{2,1,0:T(8,128)(2,1)}, bf16[4,128,128]{2,1,0:T(8,128)(2,1)S(1)}) custom-call(s32[5]{0:T(128)S(1)} %stack.30.place, bf16[512,2176]{1,0:T(8,128)(2,1)S(1)} %bitcast.19, bf16[128,2048]{1,0:T(8,128)(2,1)} %constant_dynamic-update-slice_fusion.mine, bf16[128,2048]{1,0:T(8,128)(2,1)} %collective-permute-done.3.theirs, ...), custom_call_target="tpu_custom_call" | custom-call | flops 536870912 | bytes 4194304 | tf_op jit(solution)/shard_map/pallas_call | solution.py:228
  52.8 1.3 collective-permute-start.5
  54.1 6.0 %all-to-all-start.1 = ((bf16[4,128,128]{2,1,0:T(8,128)(2,1)}), bf16[4,128,128]{2,1,0:T(8,128)(2,1)}, u32[]{:S(2)}, u32[]{:S(2)}) async-start(bf16[4,128,128]{2,1,0:T(8,128)(2,1)} %copy-done.31), calls=%async_computation.1 | async-start | bytes 262144 | tf_op jit(solution)/shard_map/all_to_all | solution.py:344
  61.9 2.2 %shard_map.88.refs_2_.q = bf16[4,128,256]{2,1,0:T(8,128)(2,1)S(1)} custom-call(bf16[512,2176]{1,0:T(8,128)(2,1)S(1)} %bitcast.20, bf16[4096,128]{1,0:T(8,128)(2,1)S(1)} %bitcast.25, bf16[4096,128]{1,0:T(8,128)(2,1)} %collective-permute-done.wb.qo_c, f32[4,128,128]{2,1,0:T(8,128)S(1)} %get-tuple-element.37.cos, f32[4,128,128]{2,1,0:T(8,128)S(1)} %copy-done.2), custom_call_target="tpu_custom_call" | custom-call | flops 536870912 | bytes 4194304 | tf_op jit(solution)/shard_map/pallas_call | solution.py:240
  64.8 1.7 shard_map.90.refs_3_
  66.5 12.0 %collective-permute-start.8 = (bf16[128,512]{1,0:T(8,128)(2,1)}, bf16[128,512]{1,0:T(8,128)(2,1)}, u32[]{:S(2)}, u32[]{:S(2)}) collective-permute-start(bf16[128,512]{1,0:T(8,128)(2,1)} %shard_map.90.refs_3_), channel_id=1, source_target_pairs={{0,8},{16,24},{32,40},{48,56},{64,72},{80,88},{96,104},{112,120},{... | collective-permute-start | bytes 393224 | tf_op jit(solution)/shard_map/ppermute | solution.py:393
  79.3 1.4 collective-permute-done.8
  80.8 1.7 add.71.refs_2_
  83.0 1.5 collective-permute-start.11
  84.5 7.1 %collective-permute-start.10 = (bf16[1024,128]{1,0:T(8,128)(2,1)}, bf16[1024,128]{1,0:T(8,128)(2,1)S(1)}, u32[]{:S(2)}, u32[]{:S(2)}) collective-permute-start(bf16[1024,128]{1,0:T(8,128)(2,1)} %get-tuple-element.23), channel_id=1, source_target_pairs={{128,0},{0,128},{129,1},{1,129},{130,2},{2,130},{131,3},{3,131},{1... | collective-permute-start | bytes 786440 | tf_op jit(solution)/shard_map/ppermute | solution.py:39
  91.6 1.6 collective-permute-start.12
  94.2 12.6 %shard_map.93.refs_4_.near = bf16[4,128,256]{2,1,0:T(8,128)(2,1)S(1)} custom-call(s32[5]{0:T(128)S(1)} %copy-done.34, bf16[4,128,256]{2,1,0:T(8,128)(2,1)S(1)} %copy-done.7, bf16[4,128,256]{2,1,0:T(8,128)(2,1)} %get-tuple-element.18.kv, bf16[4,128,256]{2,1,0:T(8,128)(2,1)S(1)} %collective-permute-done.4.kv_c, bf16[4,128,256]{2,1,0:T(8,128)(2,1)} %get-tuple-element.21.before, ...), custom_call_target="tpu_custom_call" | custom-call | flops 3489660928 | bytes 33554432 | tf_op jit(solution)/shard_map/pallas_call | solution.py:258
  106.8 1.8 slice.28
  109.3 2.4 %shard_map.95.refs_0_ = bf16[4,128,256]{2,1,0:T(8,128)(2,1)S(1)} custom-call(bf16[512,2176]{1,0:T(8,128)(2,1)S(1)} %bitcast.21, bf16[3072,128]{1,0:T(8,128)(2,1)} %get-tuple-element.22.wa.z1, bf16[3072,128]{1,0:T(8,128)(2,1)S(1)} %collective-permute-done.9.wb.z1c, f32[4,128,128]{2,1,0:T(8,128)S(1)} %get-tuple-element.37.cos, f32[4,128,128]{2,1,0:T(8,128)S(1)} %copy-done.3), custom_call_target="tpu_custom_call" | custom-call | flops 536870912 | bytes 4194304 | tf_op jit(solution)/shard_map/pallas_call | solution.py:240
  113.2 1.9 %pad_maximum_fusion = bf16[2048,128]{1,0:T(8,128)(2,1)} fusion(bf16[1024,128]{1,0:T(8,128)(2,1)} %get-tuple-element.27.z2, bf16[1024,128]{1,0:T(8,128)(2,1)} %slice.28), kind=kLoop, calls=%fused_computation.3 | loop fusion | flops 1048576 | bytes 1048576 | tf_op jit(solution)/shard_map/concatenate | solution.py:408
  115.8 1.6 collective-permute-start.14
  117.6 1.3 collective-permute-start.18
  119.8 12.5 %shard_map.97.far.refs_2_ = bf16[4,128,256]{2,1,0:T(8,128)(2,1)S(1)} custom-call(s32[5]{0:T(128)S(1)} %stack.32.place, bf16[4,128,256]{2,1,0:T(8,128)(2,1)S(1)} %copy-done.22, bf16[4,128,256]{2,1,0:T(8,128)(2,1)} %get-tuple-element.18.kv, bf16[4,128,256]{2,1,0:T(8,128)(2,1)S(1)} %copy-done.36, bf16[4,128,256]{2,1,0:T(8,128)(2,1)} %get-tuple-element.21.before, ...), custom_call_target="tpu_custom_call" | custom-call | flops 3489660928 | bytes 33554432 | tf_op jit(solution)/shard_map/pallas_call | solution.py:258
  135.7 1.3 collective-permute-start.20
  140.5 2.5 %shard_map.98.base = f32[256,2048]{1,0:T(8,128)S(1)} custom-call(bf16[4,128,256]{2,1,0:T(8,128)(2,1)S(1)} %copy-done.20, bf16[4,128,256]{2,1,0:T(8,128)(2,1)S(1)} %copy-done.17, bf16[4096,128]{1,0:T(8,128)(2,1)S(1)} %bitcast.26, bf16[4096,128]{1,0:T(8,128)(2,1)} %collective-permute-done.wb.qo_c, bf16[3072,128]{1,0:T(8,128)(2,1)} %get-tuple-element.22.wa.z1, ...), custom_call_target="tpu_custom_call" | custom-call | flops 536870912 | bytes 4194304 | tf_op jit(solution)/shard_map/pallas_call | solution.py:295
  143.7 2.1 %shard_map.100 = (bf16[128,2048]{1,0:T(8,128)(2,1)S(1)}, bf16[128,2048]{1,0:T(8,128)(2,1)S(1)}) custom-call(s32[5]{0:T(128)S(1)} %copy-done.34, bf16[128,2048]{1,0:T(8,128)(2,1)S(1)} %bitcast.28, f32[256,2048]{1,0:T(8,128)S(1)} %shard_map.98.base, bf16[2,128,256]{2,1,0:T(8,128)(2,1)S(1)} %copy-done.28, bf16[2,128,256]{2,1,0:T(8,128)(2,1)S(1)} %collective-permute-done.15.far, ...), custom_call_target="tpu_custom_call" | custom-call | flops 536870912 | bytes 4194304 | tf_op jit(solution)/shard_map/pallas_call | solution.py:307
  145.8 2.0 %collective-permute-start.21 = (bf16[128,2048]{1,0:T(8,128)(2,1)S(1)}, bf16[128,2048]{1,0:T(8,128)(2,1)S(1)}, u32[]{:S(2)}, u32[]{:S(2)}) collective-permute-start(bf16[128,2048]{1,0:T(8,128)(2,1)S(1)} %get-tuple-element.32), channel_id=1, source_target_pairs={{0,33},{32,1},{64,97},{96,65},{1,34},{33,2},{65,98},{97,66},{2,35}... | collective-permute-start | bytes 1572872 | tf_op jit(solution)/shard_map/ppermute | solution.py:421
  147.8 17.7 %collective-permute-done.21 = bf16[128,2048]{1,0:T(8,128)(2,1)S(1)} collective-permute-done((bf16[128,2048]{1,0:T(8,128)(2,1)S(1)}, bf16[128,2048]{1,0:T(8,128)(2,1)S(1)}, u32[]{:S(2)}, u32[]{:S(2)}) %collective-permute-start.21) | collective-permute-done | bytes 524320 | tf_op jit(solution)/shard_map/ppermute | solution.py:421
  165.6 12.3 %collective-permute-done.22 = bf16[128,2048]{1,0:T(8,128)(2,1)S(1)} collective-permute-done((bf16[128,2048]{1,0:T(8,128)(2,1)S(1)}, bf16[128,2048]{1,0:T(8,128)(2,1)S(1)}, u32[]{:S(2)}, u32[]{:S(2)}) %collective-permute-start.22) | collective-permute-done | bytes 524320 | tf_op jit(solution)/shard_map/ppermute | solution.py:421
  (146 shorter events, 30.0 us)
Async XLA Ops:
  5.5 42.8 %all-to-all-start = ((bf16[4,128,2176]{2,1,0:T(8,128)(2,1)}), bf16[4,128,2176]{2,1,0:T(8,128)(2,1)S(1)}, u32[]{:S(2)}, u32[]{:S(2)}) async-start(bf16[4,128,2176]{2,1,0:T(8,128)(2,1)} %copy-done), calls=%async_computation | async-start | bytes 4456448 | tf_op jit(solution)/shard_map/all_to_all | solution.py:344
  10.4 30.4 %collective-permute-start.1 = (bf16[64,2048]{1,0:T(8,128)(2,1)}, bf16[64,2048]{1,0:T(8,128)(2,1)}, u32[]{:S(2)}, u32[]{:S(2)}) collective-permute-start(bf16[64,2048]{1,0:T(8,128)(2,1)} %bitcast.11), channel_id=1, source_target_pairs={{0,0},{16,32},{32,64},{48,96},{64,16},{80,48},{96,80},{112,112},{1... | collective-permute-start | bytes 786440 | tf_op jit(solution)/shard_map/ppermute | solution.py:367
  13.8 28.7 %collective-permute-start.2 = (bf16[64,2048]{1,0:T(8,128)(2,1)}, bf16[64,2048]{1,0:T(8,128)(2,1)S(1)}, u32[]{:S(2)}, u32[]{:S(2)}) collective-permute-start(bf16[64,2048]{1,0:T(8,128)(2,1)} %bitcast.11), channel_id=1, source_target_pairs={{0,128},{16,160},{32,192},{48,224},{64,144},{80,176},{96,208},{112... | collective-permute-start | bytes 786440 | tf_op jit(solution)/shard_map/ppermute | solution.py:366
  16.0 28.9 %copy-start.41 = (f32[1,8]{1,0:T(1,128)S(1)}, f32[1,8]{1,0:T(1,128)}, u32[]{:S(2)}) copy-start(f32[1,8]{1,0:T(1,128)} %param.13) | copy-start | bytes 100
  16.3 44.6 %collective-permute-start = (bf16[4096,128]{1,0:T(8,128)(2,1)S(1)}, bf16[4096,128]{1,0:T(8,128)(2,1)}, u32[]{:S(2)}, u32[]{:S(2)}) collective-permute-start(bf16[4096,128]{1,0:T(8,128)(2,1)S(1)} %bitcast.22), channel_id=1, source_target_pairs={{16,0},{0,16},{17,1},{1,17},{18,2},{2,18},{19,3},{3,19},{20,4},{4,... | collective-permute-start | bytes 3145736 | tf_op jit(solution)/shard_map/ppermute | solution.py:39
  18.0 64.4 %collective-permute-start.7 = (bf16[3072,128]{1,0:T(8,128)(2,1)}, bf16[3072,128]{1,0:T(8,128)(2,1)}, u32[]{:S(2)}, u32[]{:S(2)}) collective-permute-start(bf16[3072,128]{1,0:T(8,128)(2,1)} %slice.30), channel_id=1, source_target_pairs={{128,0},{0,128},{129,1},{1,129},{130,2},{2,130},{131,3},{3,131},{1... | collective-permute-start | bytes 2359304 | tf_op jit(solution)/shard_map/ppermute | solution.py:39
  43.2 5.0 %collective-permute-start.3 = (bf16[128,2048]{1,0:T(8,128)(2,1)}, bf16[128,2048]{1,0:T(8,128)(2,1)}, u32[]{:S(2)}, u32[]{:S(2)}) collective-permute-start(bf16[128,2048]{1,0:T(8,128)(2,1)} %constant_dynamic-update-slice_fusion.mine), channel_id=1, source_target_pairs={{16,0},{0,16},{17,1},{1,17},{18,2},{2,18},{19,3},{3,19},{20,4},{4,... | collective-permute-start | bytes 1572872 | tf_op jit(solution)/shard_map/ppermute | solution.py:39
  52.8 25.7 %collective-permute-start.5 = (bf16[4,128,256]{2,1,0:T(8,128)(2,1)}, bf16[4,128,256]{2,1,0:T(8,128)(2,1)}, u32[]{:S(2)}, u32[]{:S(2)}) collective-permute-start(bf16[4,128,256]{2,1,0:T(8,128)(2,1)} %get-tuple-element.18.kv), channel_id=1, source_target_pairs={{0,128},{1,129},{2,130},{3,131},{4,132},{5,133},{6,134},{7,135},{8... | collective-permute-start | bytes 786440 | tf_op jit(solution)/shard_map/ppermute | solution.py:378
  54.1 10.7 %all-to-all-start.1 = ((bf16[4,128,128]{2,1,0:T(8,128)(2,1)}), bf16[4,128,128]{2,1,0:T(8,128)(2,1)}, u32[]{:S(2)}, u32[]{:S(2)}) async-start(bf16[4,128,128]{2,1,0:T(8,128)(2,1)} %copy-done.31), calls=%async_computation.1 | async-start | bytes 262144 | tf_op jit(solution)/shard_map/all_to_all | solution.py:344
  66.5 14.3 %collective-permute-start.8 = (bf16[128,512]{1,0:T(8,128)(2,1)}, bf16[128,512]{1,0:T(8,128)(2,1)}, u32[]{:S(2)}, u32[]{:S(2)}) collective-permute-start(bf16[128,512]{1,0:T(8,128)(2,1)} %shard_map.90.refs_3_), channel_id=1, source_target_pairs={{0,8},{16,24},{32,40},{48,56},{64,72},{80,88},{96,104},{112,120},{... | collective-permute-start | bytes 393224 | tf_op jit(solution)/shard_map/ppermute | solution.py:393
  78.5 14.8 %copy-start.34 = (s32[5]{0:T(128)S(1)}, s32[5]{0:T(128)}, u32[]{:S(2)}) copy-start(s32[5]{0:T(128)} %copy-done.33) | copy-start | bytes 64
  78.5 3.9 %collective-permute-start.6 = (bf16[4,128,256]{2,1,0:T(8,128)(2,1)}, bf16[4,128,256]{2,1,0:T(8,128)(2,1)}, u32[]{:S(2)}, u32[]{:S(2)}) collective-permute-start(bf16[4,128,256]{2,1,0:T(8,128)(2,1)} %get-tuple-element.21.before), channel_id=1, source_target_pairs={{16,0},{0,16},{17,1},{1,17},{18,2},{2,18},{19,3},{3,19},{20,4},{4,... | collective-permute-start | bytes 786440 | tf_op jit(solution)/shard_map/ppermute | solution.py:39
  82.4 26.8 %collective-permute-start.9 = (bf16[3072,128]{1,0:T(8,128)(2,1)}, bf16[3072,128]{1,0:T(8,128)(2,1)S(1)}, u32[]{:S(2)}, u32[]{:S(2)}) collective-permute-start(bf16[3072,128]{1,0:T(8,128)(2,1)} %get-tuple-element.22.wa.z1), channel_id=1, source_target_pairs={{16,0},{0,16},{17,1},{1,17},{18,2},{2,18},{19,3},{3,19},{20,4},{4,... | collective-permute-start | bytes 2359304 | tf_op jit(solution)/shard_map/ppermute | solution.py:39
  82.5 10.7 %collective-permute-start.4 = (bf16[4,128,256]{2,1,0:T(8,128)(2,1)}, bf16[4,128,256]{2,1,0:T(8,128)(2,1)S(1)}, u32[]{:S(2)}, u32[]{:S(2)}) collective-permute-start(bf16[4,128,256]{2,1,0:T(8,128)(2,1)} %get-tuple-element.18.kv), channel_id=1, source_target_pairs={{16,0},{0,16},{17,1},{1,17},{18,2},{2,18},{19,3},{3,19},{20,4},{4,... | collective-permute-start | bytes 786440 | tf_op jit(solution)/shard_map/ppermute | solution.py:39
  83.0 30.2 %collective-permute-start.11 = (bf16[2048,128]{1,0:T(8,128)(2,1)}, bf16[2048,128]{1,0:T(8,128)(2,1)}, u32[]{:S(2)}, u32[]{:S(2)}) collective-permute-start(bf16[2048,128]{1,0:T(8,128)(2,1)} %get-tuple-element.24), channel_id=1, source_target_pairs={{0,96},{32,64},{64,32},{96,0},{1,97},{33,65},{65,33},{97,1},{2,98}... | collective-permute-start | bytes 1572872 | tf_op jit(solution)/shard_map/ppermute | solution.py:340
  84.5 28.0 %collective-permute-start.10 = (bf16[1024,128]{1,0:T(8,128)(2,1)}, bf16[1024,128]{1,0:T(8,128)(2,1)S(1)}, u32[]{:S(2)}, u32[]{:S(2)}) collective-permute-start(bf16[1024,128]{1,0:T(8,128)(2,1)} %get-tuple-element.23), channel_id=1, source_target_pairs={{128,0},{0,128},{129,1},{1,129},{130,2},{2,130},{131,3},{3,131},{1... | collective-permute-start | bytes 786440 | tf_op jit(solution)/shard_map/ppermute | solution.py:39
  91.6 17.6 %copy-start.3 = (f32[4,128,128]{2,1,0:T(8,128)S(1)}, f32[4,128,128]{2,1,0:T(8,128)}, u32[]{:S(2)}) copy-start(f32[4,128,128]{2,1,0:T(8,128)} %get-tuple-element.38.sin) | copy-start | bytes 786436
  91.6 16.9 %collective-permute-start.12 = (bf16[128,512]{1,0:T(8,128)(2,1)}, bf16[128,512]{1,0:T(8,128)(2,1)S(1)}, u32[]{:S(2)}, u32[]{:S(2)}) collective-permute-start(bf16[128,512]{1,0:T(8,128)(2,1)} %get-tuple-element.25), channel_id=1, source_target_pairs={{0,4},{8,12},{16,20},{24,28},{32,36},{40,44},{48,52},{56,60},{64,6... | collective-permute-start | bytes 393224 | tf_op jit(solution)/shard_map/ppermute | solution.py:393
  94.2 12.6 %copy-start.35 = (bf16[4,128,256]{2,1,0:T(8,128)(2,1)}, bf16[4,128,256]{2,1,0:T(8,128)(2,1)S(1)}, u32[]{:S(2)}) copy-start(bf16[4,128,256]{2,1,0:T(8,128)(2,1)S(1)} %collective-permute-done.4.kv_c) | copy-start | bytes 786436
  94.2 14.4 %copy-start.40 = (bf16[128,512]{1,0:T(8,128)(2,1)S(1)}, bf16[128,512]{1,0:T(8,128)(2,1)}, u32[]{:S(2)}) copy-start(bf16[128,512]{1,0:T(8,128)(2,1)} %get-tuple-element.25) | copy-start | bytes 393220
  112.5 6.4 %copy-start.36 = (bf16[4,128,256]{2,1,0:T(8,128)(2,1)S(1)}, bf16[4,128,256]{2,1,0:T(8,128)(2,1)}, u32[]{:S(2)}) copy-start(bf16[4,128,256]{2,1,0:T(8,128)(2,1)} %copy-done.35) | copy-start | bytes 786436
  115.1 18.0 %collective-permute-start.17 = (bf16[2048,128]{1,0:T(8,128)(2,1)}, bf16[2048,128]{1,0:T(8,128)(2,1)S(1)}, u32[]{:S(2)}, u32[]{:S(2)}) collective-permute-start(bf16[2048,128]{1,0:T(8,128)(2,1)} %pad_maximum_fusion), channel_id=1, source_target_pairs={{0,96},{32,64},{64,32},{96,0},{1,97},{33,65},{65,33},{97,1},{2,98}... | collective-permute-start | bytes 1572872 | tf_op jit(solution)/shard_map/ppermute | solution.py:340
  115.7 18.2 %collective-permute-start.16 = (bf16[2048,128]{1,0:T(8,128)(2,1)}, bf16[2048,128]{1,0:T(8,128)(2,1)S(1)}, u32[]{:S(2)}, u32[]{:S(2)}) collective-permute-start(bf16[2048,128]{1,0:T(8,128)(2,1)} %get-tuple-element.28.o_b), channel_id=1, source_target_pairs={{16,0},{0,16},{17,1},{1,17},{18,2},{2,18},{19,3},{3,19},{20,4},{4,... | collective-permute-start | bytes 1572872 | tf_op jit(solution)/shard_map/ppermute | solution.py:39
  115.8 17.3 %collective-permute-start.14 = (bf16[2,128,256]{2,1,0:T(8,128)(2,1)S(1)}, bf16[2,128,256]{2,1,0:T(8,128)(2,1)S(1)}, u32[]{:S(2)}, u32[]{:S(2)}) collective-permute-start(bf16[2,128,256]{2,1,0:T(8,128)(2,1)S(1)} %slice.32), channel_id=1, source_target_pairs={{0,96},{32,64},{64,32},{96,0},{1,97},{33,65},{65,33},{97,1},{2,98}... | collective-permute-start | bytes 393224 | tf_op jit(solution)/shard_map/ppermute | solution.py:340
  117.3 15.8 %collective-permute-start.13 = (bf16[1024,128]{1,0:T(8,128)(2,1)}, bf16[1024,128]{1,0:T(8,128)(2,1)S(1)}, u32[]{:S(2)}, u32[]{:S(2)}) collective-permute-start(bf16[1024,128]{1,0:T(8,128)(2,1)} %get-tuple-element.27.z2), channel_id=1, source_target_pairs={{16,0},{0,16},{17,1},{1,17},{18,2},{2,18},{19,3},{3,19},{20,4},{4,... | collective-permute-start | bytes 786440 | tf_op jit(solution)/shard_map/ppermute | solution.py:39
  117.6 14.8 %collective-permute-start.18 = (bf16[128,512]{1,0:T(8,128)(2,1)}, bf16[128,512]{1,0:T(8,128)(2,1)S(1)}, u32[]{:S(2)}, u32[]{:S(2)}) collective-permute-start(bf16[128,512]{1,0:T(8,128)(2,1)} %get-tuple-element.29), channel_id=1, source_target_pairs={{0,2},{4,6},{8,10},{12,14},{16,18},{20,22},{24,26},{28,30},{32,34}... | collective-permute-start | bytes 393224 | tf_op jit(solution)/shard_map/ppermute | solution.py:393
  119.8 12.6 %copy-start.39 = (bf16[128,512]{1,0:T(8,128)(2,1)S(1)}, bf16[128,512]{1,0:T(8,128)(2,1)}, u32[]{:S(2)}) copy-start(bf16[128,512]{1,0:T(8,128)(2,1)} %get-tuple-element.29) | copy-start | bytes 393220
  135.5 8.2 %collective-permute-start.19 = (bf16[2048,128]{1,0:T(8,128)(2,1)}, bf16[2048,128]{1,0:T(8,128)(2,1)S(1)}, u32[]{:S(2)}, u32[]{:S(2)}) collective-permute-start(bf16[2048,128]{1,0:T(8,128)(2,1)} %get-tuple-element.30.o_zb), channel_id=1, source_target_pairs={{16,0},{0,16},{17,1},{1,17},{18,2},{2,18},{19,3},{3,19},{20,4},{4,... | collective-permute-start | bytes 1572872 | tf_op jit(solution)/shard_map/ppermute | solution.py:39
  135.7 7.3 %collective-permute-start.20 = (bf16[128,512]{1,0:T(8,128)(2,1)}, bf16[128,512]{1,0:T(8,128)(2,1)S(1)}, u32[]{:S(2)}, u32[]{:S(2)}) collective-permute-start(bf16[128,512]{1,0:T(8,128)(2,1)} %get-tuple-element.31), channel_id=1, source_target_pairs={{0,1},{2,3},{4,5},{6,7},{8,9},{10,11},{12,13},{14,15},{16,17},{18,... | collective-permute-start | bytes 393224 | tf_op jit(solution)/shard_map/ppermute | solution.py:393
  138.0 5.7 %collective-permute-start.15 = (bf16[2,128,256]{2,1,0:T(8,128)(2,1)S(1)}, bf16[2,128,256]{2,1,0:T(8,128)(2,1)S(1)}, u32[]{:S(2)}, u32[]{:S(2)}) collective-permute-start(bf16[2,128,256]{2,1,0:T(8,128)(2,1)S(1)} %slice.33), channel_id=1, source_target_pairs={{0,96},{32,64},{64,32},{96,0},{1,97},{33,65},{65,33},{97,1},{2,98}... | collective-permute-start | bytes 393224 | tf_op jit(solution)/shard_map/ppermute | solution.py:340
  145.8 19.7 %collective-permute-start.21 = (bf16[128,2048]{1,0:T(8,128)(2,1)S(1)}, bf16[128,2048]{1,0:T(8,128)(2,1)S(1)}, u32[]{:S(2)}, u32[]{:S(2)}) collective-permute-start(bf16[128,2048]{1,0:T(8,128)(2,1)S(1)} %get-tuple-element.32), channel_id=1, source_target_pairs={{0,33},{32,1},{64,97},{96,65},{1,34},{33,2},{65,98},{97,66},{2,35}... | collective-permute-start | bytes 1572872 | tf_op jit(solution)/shard_map/ppermute | solution.py:421
  147.8 30.1 %collective-permute-start.22 = (bf16[128,2048]{1,0:T(8,128)(2,1)S(1)}, bf16[128,2048]{1,0:T(8,128)(2,1)S(1)}, u32[]{:S(2)}, u32[]{:S(2)}) collective-permute-start(bf16[128,2048]{1,0:T(8,128)(2,1)S(1)} %get-tuple-element.33), channel_id=1, source_target_pairs={{0,1},{1,2},{2,3},{3,4},{4,5},{5,6},{6,7},{7,8},{8,9},{9,10},{10,1... | collective-permute-start | bytes 1572872 | tf_op jit(solution)/shard_map/ppermute | solution.py:421
  (35 other events, 76.7 us)

commit v2 on v0

--- a/solution.py
+++ b/solution.py
@@ -14,7 +14,7 @@
 rope_base = 500000.0
 F32 = jnp.float32
 BF16 = jnp.bfloat16
-CHUNK = 512
+CHUNK = 1024
 
 
 def prepare_kernel(acts, gain, first, out):

time: 176 us -> 174 us (0.989)
  Pallas kernels: 40.2 us -> 37.8 us
    pallas_call x2, Pallas kernels: 25.1 us -> 22.7 us  [attend(): pl.pallas_call(attend_kernel, out_shape=jax.ShapeDtypeStruct((4, 128, 256...]
  transfers between devices with their start and end apart: 26 -> 26, of which waited for: 6 -> 6; matrix products, arithmetic and copies ran while one was open for 7% -> 8% of each run, Pallas kernels for 21% -> 20%
where the time goes in v2:
time: 174 us; the launch traced here: 173 us
  waiting for transfers between devices  52.4 us (30%)
  starting transfers between devices  49.1 us (28%)
  Pallas kernels  37.8 us (22%)
  local copies, waits for them, and re-layouts  24.9 us (14%)
  other arithmetic  7.15 us (4%)
    pallas_call x2, Pallas kernels, attend(): pl.pallas_call(attend_kernel, out_shape=jax.ShapeDtypeStruct((4, 128, 256...  22.7 us
    unnamed x81, local copies, waits for them, and re-layouts  19.1 us
    ppermute x1, waiting for transfers between devices, per_device(): kv_a = lax.ppermute(w_kv, SEQ, home)  17.4 us
    ppermute x1, waiting for transfers between devices, per_device(): lax.ppermute(theirs, ('y',) + PIPE, across)  16.8 us
    ppermute x5, starting transfers between devices, sent_on(): return sum([lax.ppermute(x, PIPE, pairs) for pairs in rounds], x)  14.9 us
    ppermute x1, waiting for transfers between devices, per_device(): lax.ppermute(mine, PIPE, onward)  12.3 us
    all_to_all x2, starting transfers between devices, swap(): return lax.all_to_all(x, 'y', 0, 0)  10.9 us
    ppermute x10, starting transfers between devices, pull(): return lax.ppermute(x, axis, [((i + by) % n, i) for i in range(n)])  10.2 us
  transfers between devices with their start and end apart: 26, of which 6 were waited for; matrix products, arithmetic and copies ran while one was open for 8% of the time, Pallas kernels for 20%

profile of v2, /device:TPU:136, one launch (start us, length us, event | category | flops | bytes accessed | tf_op | source)
XLA Modules:
  0.0 172.5 jit_solution(11601795691689327129)
XLA Ops:
  4.1 1.3 copy-done
  5.5 4.9 %all-to-all-start = ((bf16[4,128,2176]{2,1,0:T(8,128)(2,1)}), bf16[4,128,2176]{2,1,0:T(8,128)(2,1)S(1)}, u32[]{:S(2)}, u32[]{:S(2)}) async-start(bf16[4,128,2176]{2,1,0:T(8,128)(2,1)} %copy-done), calls=%async_computation | async-start | bytes 4456448 | tf_op jit(solution)/shard_map/all_to_all | solution.py:344
  10.4 3.4 %collective-permute-start.1 = (bf16[64,2048]{1,0:T(8,128)(2,1)}, bf16[64,2048]{1,0:T(8,128)(2,1)}, u32[]{:S(2)}, u32[]{:S(2)}) collective-permute-start(bf16[64,2048]{1,0:T(8,128)(2,1)} %bitcast.11), channel_id=1, source_target_pairs={{0,0},{16,32},{32,64},{48,96},{64,16},{80,48},{96,80},{112,112},{1... | collective-permute-start | bytes 786440 | tf_op jit(solution)/shard_map/ppermute | solution.py:367
  18.0 5.4 %collective-permute-start.7 = (bf16[3072,128]{1,0:T(8,128)(2,1)}, bf16[3072,128]{1,0:T(8,128)(2,1)}, u32[]{:S(2)}, u32[]{:S(2)}) collective-permute-start(bf16[3072,128]{1,0:T(8,128)(2,1)} %slice.30), channel_id=1, source_target_pairs={{128,0},{0,128},{129,1},{1,129},{130,2},{2,130},{131,3},{3,131},{1... | collective-permute-start | bytes 2359304 | tf_op jit(solution)/shard_map/ppermute | solution.py:39
  23.4 17.4 %collective-permute-done.1 = bf16[64,2048]{1,0:T(8,128)(2,1)} collective-permute-done((bf16[64,2048]{1,0:T(8,128)(2,1)}, bf16[64,2048]{1,0:T(8,128)(2,1)}, u32[]{:S(2)}, u32[]{:S(2)}) %collective-permute-start.1) | collective-permute-done | bytes 262176 | tf_op jit(solution)/shard_map/ppermute | solution.py:367
  40.8 1.7 constant_dynamic-update-slice_fusion.1
  43.2 1.1 collective-permute-start.3
  47.1 1.2 pad_maximum_fusion.1
  49.2 3.0 %shard_map.89 = (bf16[4,128,256]{2,1,0:T(8,128)(2,1)}, bf16[4,128,128]{2,1,0:T(8,128)(2,1)S(1)}) custom-call(s32[5]{0:T(128)S(1)} %stack.30.place, bf16[512,2176]{1,0:T(8,128)(2,1)S(1)} %bitcast.19, bf16[128,2048]{1,0:T(8,128)(2,1)} %constant_dynamic-update-slice_fusion.mine, bf16[128,2048]{1,0:T(8,128)(2,1)} %collective-permute-done.3.theirs, ...), custom_call_target="tpu_custom_call" | custom-call | flops 536870912 | bytes 4194304 | tf_op jit(solution)/shard_map/pallas_call | solution.py:228
  52.8 1.3 collective-permute-start.5
  54.1 6.0 %all-to-all-start.1 = ((bf16[4,128,128]{2,1,0:T(8,128)(2,1)}), bf16[4,128,128]{2,1,0:T(8,128)(2,1)}, u32[]{:S(2)}, u32[]{:S(2)}) async-start(bf16[4,128,128]{2,1,0:T(8,128)(2,1)} %copy-done.28), calls=%async_computation.1 | async-start | bytes 262144 | tf_op jit(solution)/shard_map/all_to_all | solution.py:344
  61.9 2.2 %shard_map.88.refs_2_.q = bf16[4,128,256]{2,1,0:T(8,128)(2,1)S(1)} custom-call(bf16[512,2176]{1,0:T(8,128)(2,1)S(1)} %bitcast.20, bf16[4096,128]{1,0:T(8,128)(2,1)S(1)} %bitcast.25, bf16[4096,128]{1,0:T(8,128)(2,1)} %collective-permute-done.wb.qo_c, f32[4,128,128]{2,1,0:T(8,128)S(1)} %get-tuple-element.37.cos, f32[4,128,128]{2,1,0:T(8,128)S(1)} %copy-done.2), custom_call_target="tpu_custom_call" | custom-call | flops 536870912 | bytes 4194304 | tf_op jit(solution)/shard_map/pallas_call | solution.py:240
  64.8 1.7 shard_map.90.refs_3_.refs_2_
  66.5 4.3 %collective-permute-done.5.refs_0_ = bf16[4,128,256]{2,1,0:T(8,128)(2,1)} collective-permute-done((bf16[4,128,256]{2,1,0:T(8,128)(2,1)}, bf16[4,128,256]{2,1,0:T(8,128)(2,1)}, u32[]{:S(2)}, u32[]{:S(2)}) %collective-permute-start.5) | collective-permute-done | bytes 262176 | tf_op jit(solution)/shard_map/ppermute | solution.py:378
  73.1 2.6 %collective-permute-start.10 = (bf16[2048,128]{1,0:T(8,128)(2,1)}, bf16[2048,128]{1,0:T(8,128)(2,1)}, u32[]{:S(2)}, u32[]{:S(2)}) collective-permute-start(bf16[2048,128]{1,0:T(8,128)(2,1)} %get-tuple-element.24), channel_id=1, source_target_pairs={{0,96},{32,64},{64,32},{96,0},{1,97},{33,65},{65,33},{97,1},{2,98}... | collective-permute-start | bytes 1572872 | tf_op jit(solution)/shard_map/ppermute | solution.py:340
  75.8 1.9 %collective-permute-start.9 = (bf16[1024,128]{1,0:T(8,128)(2,1)}, bf16[1024,128]{1,0:T(8,128)(2,1)S(1)}, u32[]{:S(2)}, u32[]{:S(2)}) collective-permute-start(bf16[1024,128]{1,0:T(8,128)(2,1)} %get-tuple-element.23), channel_id=1, source_target_pairs={{128,0},{0,128},{129,1},{1,129},{130,2},{2,130},{131,3},{3,131},{1... | collective-permute-start | bytes 786440 | tf_op jit(solution)/shard_map/ppermute | solution.py:39
  77.7 8.2 %collective-permute-start.11 = (bf16[128,512]{1,0:T(8,128)(2,1)}, bf16[128,512]{1,0:T(8,128)(2,1)S(1)}, u32[]{:S(2)}, u32[]{:S(2)}) collective-permute-start(bf16[128,512]{1,0:T(8,128)(2,1)} %get-tuple-element.25), channel_id=1, source_target_pairs={{0,2},{16,18},{32,34},{48,50},{64,66},{80,82},{96,98},{112,114},{1... | collective-permute-start | bytes 393224 | tf_op jit(solution)/shard_map/ppermute | solution.py:393
  86.9 11.3 %shard_map.93.refs_4_.near = bf16[4,128,256]{2,1,0:T(8,128)(2,1)S(1)} custom-call(s32[5]{0:T(128)S(1)} %copy-done.31, bf16[4,128,256]{2,1,0:T(8,128)(2,1)S(1)} %copy-done.7, bf16[4,128,256]{2,1,0:T(8,128)(2,1)} %get-tuple-element.18.kv, bf16[4,128,256]{2,1,0:T(8,128)(2,1)S(1)} %collective-permute-done.4.kv_c, bf16[4,128,256]{2,1,0:T(8,128)(2,1)} %get-tuple-element.21.before, ...), custom_call_target="tpu_custom_call" | custom-call | flops 3489660928 | bytes 33554432 | tf_op jit(solution)/shard_map/pallas_call | solution.py:258
  98.3 1.8 %slice.28 = bf16[1024,128]{1,0:T(8,128)(2,1)} slice(bf16[3072,128]{1,0:T(8,128)(2,1)} %get-tuple-element.22.wa.z1), slice={[2048:3072], [0:128]} | slice | bytes 524288 | tf_op jit(solution)/shard_map/slice | solution.py:406
  100.7 2.4 %shard_map.95.refs_0_ = bf16[4,128,256]{2,1,0:T(8,128)(2,1)S(1)} custom-call(bf16[512,2176]{1,0:T(8,128)(2,1)S(1)} %bitcast.21, bf16[3072,128]{1,0:T(8,128)(2,1)} %get-tuple-element.22.wa.z1, bf16[3072,128]{1,0:T(8,128)(2,1)S(1)} %collective-permute-done.8.wb.z1c, f32[4,128,128]{2,1,0:T(8,128)S(1)} %get-tuple-element.37.cos, f32[4,128,128]{2,1,0:T(8,128)S(1)} %copy-done.3), custom_call_target="tpu_custom_call" | custom-call | flops 536870912 | bytes 4194304 | tf_op jit(solution)/shard_map/pallas_call | solution.py:240
  104.6 1.9 %pad_maximum_fusion = bf16[2048,128]{1,0:T(8,128)(2,1)} fusion(bf16[1024,128]{1,0:T(8,128)(2,1)} %get-tuple-element.27.z2, bf16[1024,128]{1,0:T(8,128)(2,1)} %slice.28), kind=kLoop, calls=%fused_computation.3 | loop fusion | flops 1048576 | bytes 1048576 | tf_op jit(solution)/shard_map/concatenate | solution.py:406
  106.7 2.1 %collective-permute-start.13 = (bf16[2,128,256]{2,1,0:T(8,128)(2,1)S(1)}, bf16[2,128,256]{2,1,0:T(8,128)(2,1)S(1)}, u32[]{:S(2)}, u32[]{:S(2)}) collective-permute-start(bf16[2,128,256]{2,1,0:T(8,128)(2,1)S(1)} %slice.32), channel_id=1, source_target_pairs={{0,96},{32,64},{64,32},{96,0},{1,97},{33,65},{65,33},{97,1},{2,98}... | collective-permute-start | bytes 393224 | tf_op jit(solution)/shard_map/ppermute | solution.py:340
  109.0 1.3 collective-permute-start.17
  111.2 11.3 %shard_map.97.far.refs_2_ = bf16[4,128,256]{2,1,0:T(8,128)(2,1)S(1)} custom-call(s32[5]{0:T(128)S(1)} %stack.32.place, bf16[4,128,256]{2,1,0:T(8,128)(2,1)S(1)} %copy-done.19, bf16[4,128,256]{2,1,0:T(8,128)(2,1)} %get-tuple-element.18.kv, bf16[4,128,256]{2,1,0:T(8,128)(2,1)S(1)} %copy-done.33, bf16[4,128,256]{2,1,0:T(8,128)(2,1)} %get-tuple-element.21.before, ...), custom_call_target="tpu_custom_call" | custom-call | flops 3489660928 | bytes 33554432 | tf_op jit(solution)/shard_map/pallas_call | solution.py:258
  125.2 1.9 %collective-permute-start.19 = (bf16[128,512]{1,0:T(8,128)(2,1)}, bf16[128,512]{1,0:T(8,128)(2,1)S(1)}, u32[]{:S(2)}, u32[]{:S(2)}) collective-permute-start(bf16[128,512]{1,0:T(8,128)(2,1)} %get-tuple-element.31), channel_id=1, source_target_pairs={{0,4},{1,5},{2,6},{3,7},{16,20},{17,21},{18,22},{19,23},{32,36},{3... | collective-permute-start | bytes 393224 | tf_op jit(solution)/shard_map/ppermute | solution.py:393
  127.1 2.2 %collective-permute-start.20 = (bf16[128,512]{1,0:T(8,128)(2,1)}, bf16[128,512]{1,0:T(8,128)(2,1)S(1)}, u32[]{:S(2)}, u32[]{:S(2)}) collective-permute-start(bf16[128,512]{1,0:T(8,128)(2,1)} %get-tuple-element.31), channel_id=1, source_target_pairs={{0,8},{1,9},{2,10},{3,11},{16,24},{17,25},{18,26},{19,27},{32,40},... | collective-permute-start | bytes 393224 | tf_op jit(solution)/shard_map/ppermute | solution.py:393
  129.3 1.3 collective-permute-start.21
  134.1 2.5 %shard_map.98.base = f32[256,2048]{1,0:T(8,128)S(1)} custom-call(bf16[4,128,256]{2,1,0:T(8,128)(2,1)S(1)} %copy-done.17, bf16[4,128,256]{2,1,0:T(8,128)(2,1)S(1)} %copy-done.15, bf16[4096,128]{1,0:T(8,128)(2,1)S(1)} %bitcast.26, bf16[4096,128]{1,0:T(8,128)(2,1)} %collective-permute-done.wb.qo_c, bf16[3072,128]{1,0:T(8,128)(2,1)} %get-tuple-element.22.wa.z1, ...), custom_call_target="tpu_custom_call" | custom-call | flops 536870912 | bytes 4194304 | tf_op jit(solution)/shard_map/pallas_call | solution.py:295
  137.3 2.2 %shard_map.100 = (bf16[128,2048]{1,0:T(8,128)(2,1)S(1)}, bf16[128,2048]{1,0:T(8,128)(2,1)S(1)}) custom-call(s32[5]{0:T(128)S(1)} %copy-done.31, bf16[128,2048]{1,0:T(8,128)(2,1)S(1)} %bitcast.28, f32[256,2048]{1,0:T(8,128)S(1)} %shard_map.98.base, bf16[2,128,256]{2,1,0:T(8,128)(2,1)S(1)} %copy-done.25, bf16[2,128,256]{2,1,0:T(8,128)(2,1)S(1)} %collective-permute-done.14.far, ...), custom_call_target="tpu_custom_call" | custom-call | flops 536870912 | bytes 4194304 | tf_op jit(solution)/shard_map/pallas_call | solution.py:307
  140.5 1.9 %collective-permute-start.23 = (bf16[128,2048]{1,0:T(8,128)(2,1)S(1)}, bf16[128,2048]{1,0:T(8,128)(2,1)S(1)}, u32[]{:S(2)}, u32[]{:S(2)}) collective-permute-start(bf16[128,2048]{1,0:T(8,128)(2,1)S(1)} %get-tuple-element.33), channel_id=1, source_target_pairs={{0,1},{1,2},{2,3},{3,4},{4,5},{5,6},{6,7},{7,8},{8,9},{9,10},{10,1... | collective-permute-start | bytes 1572872 | tf_op jit(solution)/shard_map/ppermute | solution.py:419
  142.4 16.8 %collective-permute-done.22 = bf16[128,2048]{1,0:T(8,128)(2,1)S(1)} collective-permute-done((bf16[128,2048]{1,0:T(8,128)(2,1)S(1)}, bf16[128,2048]{1,0:T(8,128)(2,1)S(1)}, u32[]{:S(2)}, u32[]{:S(2)}) %collective-permute-start.22) | collective-permute-done | bytes 524320 | tf_op jit(solution)/shard_map/ppermute | solution.py:419
  159.2 12.3 %collective-permute-done.23 = bf16[128,2048]{1,0:T(8,128)(2,1)S(1)} collective-permute-done((bf16[128,2048]{1,0:T(8,128)(2,1)S(1)}, bf16[128,2048]{1,0:T(8,128)(2,1)S(1)}, u32[]{:S(2)}, u32[]{:S(2)}) %collective-permute-start.23) | collective-permute-done | bytes 524320 | tf_op jit(solution)/shard_map/ppermute | solution.py:419
  (141 shorter events, 30.6 us)
Async XLA Ops:
  5.5 42.8 %all-to-all-start = ((bf16[4,128,2176]{2,1,0:T(8,128)(2,1)}), bf16[4,128,2176]{2,1,0:T(8,128)(2,1)S(1)}, u32[]{:S(2)}, u32[]{:S(2)}) async-start(bf16[4,128,2176]{2,1,0:T(8,128)(2,1)} %copy-done), calls=%async_computation | async-start | bytes 4456448 | tf_op jit(solution)/shard_map/all_to_all | solution.py:344
  10.4 30.4 %collective-permute-start.1 = (bf16[64,2048]{1,0:T(8,128)(2,1)}, bf16[64,2048]{1,0:T(8,128)(2,1)}, u32[]{:S(2)}, u32[]{:S(2)}) collective-permute-start(bf16[64,2048]{1,0:T(8,128)(2,1)} %bitcast.11), channel_id=1, source_target_pairs={{0,0},{16,32},{32,64},{48,96},{64,16},{80,48},{96,80},{112,112},{1... | collective-permute-start | bytes 786440 | tf_op jit(solution)/shard_map/ppermute | solution.py:367
  13.7 28.7 %collective-permute-start.2 = (bf16[64,2048]{1,0:T(8,128)(2,1)}, bf16[64,2048]{1,0:T(8,128)(2,1)S(1)}, u32[]{:S(2)}, u32[]{:S(2)}) collective-permute-start(bf16[64,2048]{1,0:T(8,128)(2,1)} %bitcast.11), channel_id=1, source_target_pairs={{0,128},{16,160},{32,192},{48,224},{64,144},{80,176},{96,208},{112... | collective-permute-start | bytes 786440 | tf_op jit(solution)/shard_map/ppermute | solution.py:366
  15.9 28.9 %copy-start.38 = (f32[1,8]{1,0:T(1,128)S(1)}, f32[1,8]{1,0:T(1,128)}, u32[]{:S(2)}) copy-start(f32[1,8]{1,0:T(1,128)} %param.13) | copy-start | bytes 100
  16.3 44.7 %collective-permute-start = (bf16[4096,128]{1,0:T(8,128)(2,1)S(1)}, bf16[4096,128]{1,0:T(8,128)(2,1)}, u32[]{:S(2)}, u32[]{:S(2)}) collective-permute-start(bf16[4096,128]{1,0:T(8,128)(2,1)S(1)} %bitcast.22), channel_id=1, source_target_pairs={{16,0},{0,16},{17,1},{1,17},{18,2},{2,18},{19,3},{3,19},{20,4},{4,... | collective-permute-start | bytes 3145736 | tf_op jit(solution)/shard_map/ppermute | solution.py:39
  18.0 53.6 %collective-permute-start.7 = (bf16[3072,128]{1,0:T(8,128)(2,1)}, bf16[3072,128]{1,0:T(8,128)(2,1)}, u32[]{:S(2)}, u32[]{:S(2)}) collective-permute-start(bf16[3072,128]{1,0:T(8,128)(2,1)} %slice.30), channel_id=1, source_target_pairs={{128,0},{0,128},{129,1},{1,129},{130,2},{2,130},{131,3},{3,131},{1... | collective-permute-start | bytes 2359304 | tf_op jit(solution)/shard_map/ppermute | solution.py:39
  43.2 5.0 %collective-permute-start.3 = (bf16[128,2048]{1,0:T(8,128)(2,1)}, bf16[128,2048]{1,0:T(8,128)(2,1)}, u32[]{:S(2)}, u32[]{:S(2)}) collective-permute-start(bf16[128,2048]{1,0:T(8,128)(2,1)} %constant_dynamic-update-slice_fusion.mine), channel_id=1, source_target_pairs={{16,0},{0,16},{17,1},{1,17},{18,2},{2,18},{19,3},{3,19},{20,4},{4,... | collective-permute-start | bytes 1572872 | tf_op jit(solution)/shard_map/ppermute | solution.py:39
  52.8 17.9 %collective-permute-start.5 = (bf16[4,128,256]{2,1,0:T(8,128)(2,1)}, bf16[4,128,256]{2,1,0:T(8,128)(2,1)}, u32[]{:S(2)}, u32[]{:S(2)}) collective-permute-start(bf16[4,128,256]{2,1,0:T(8,128)(2,1)} %get-tuple-element.18.kv), channel_id=1, source_target_pairs={{0,128},{1,129},{2,130},{3,131},{4,132},{5,133},{6,134},{7,135},{8... | collective-permute-start | bytes 786440 | tf_op jit(solution)/shard_map/ppermute | solution.py:378
  54.1 10.7 %all-to-all-start.1 = ((bf16[4,128,128]{2,1,0:T(8,128)(2,1)}), bf16[4,128,128]{2,1,0:T(8,128)(2,1)}, u32[]{:S(2)}, u32[]{:S(2)}) async-start(bf16[4,128,128]{2,1,0:T(8,128)(2,1)} %copy-done.28), calls=%async_computation.1 | async-start | bytes 262144 | tf_op jit(solution)/shard_map/all_to_all | solution.py:344
  66.5 19.4 %copy-start.31 = (s32[5]{0:T(128)S(1)}, s32[5]{0:T(128)}, u32[]{:S(2)}) copy-start(s32[5]{0:T(128)} %copy-done.30) | copy-start | bytes 64
  70.8 1.9 %collective-permute-start.6 = (bf16[4,128,256]{2,1,0:T(8,128)(2,1)}, bf16[4,128,256]{2,1,0:T(8,128)(2,1)}, u32[]{:S(2)}, u32[]{:S(2)}) collective-permute-start(bf16[4,128,256]{2,1,0:T(8,128)(2,1)} %get-tuple-element.21.before), channel_id=1, source_target_pairs={{16,0},{0,16},{17,1},{1,17},{18,2},{2,18},{19,3},{3,19},{20,4},{4,... | collective-permute-start | bytes 786440 | tf_op jit(solution)/shard_map/ppermute | solution.py:39
  72.6 28.1 %collective-permute-start.8 = (bf16[3072,128]{1,0:T(8,128)(2,1)}, bf16[3072,128]{1,0:T(8,128)(2,1)S(1)}, u32[]{:S(2)}, u32[]{:S(2)}) collective-permute-start(bf16[3072,128]{1,0:T(8,128)(2,1)} %get-tuple-element.22.wa.z1), channel_id=1, source_target_pairs={{16,0},{0,16},{17,1},{1,17},{18,2},{2,18},{19,3},{3,19},{20,4},{4,... | collective-permute-start | bytes 2359304 | tf_op jit(solution)/shard_map/ppermute | solution.py:39
  72.8 13.2 %collective-permute-start.4 = (bf16[4,128,256]{2,1,0:T(8,128)(2,1)}, bf16[4,128,256]{2,1,0:T(8,128)(2,1)S(1)}, u32[]{:S(2)}, u32[]{:S(2)}) collective-permute-start(bf16[4,128,256]{2,1,0:T(8,128)(2,1)} %get-tuple-element.18.kv), channel_id=1, source_target_pairs={{16,0},{0,16},{17,1},{1,17},{18,2},{2,18},{19,3},{3,19},{20,4},{4,... | collective-permute-start | bytes 786440 | tf_op jit(solution)/shard_map/ppermute | solution.py:39
  73.1 31.5 %collective-permute-start.10 = (bf16[2048,128]{1,0:T(8,128)(2,1)}, bf16[2048,128]{1,0:T(8,128)(2,1)}, u32[]{:S(2)}, u32[]{:S(2)}) collective-permute-start(bf16[2048,128]{1,0:T(8,128)(2,1)} %get-tuple-element.24), channel_id=1, source_target_pairs={{0,96},{32,64},{64,32},{96,0},{1,97},{33,65},{65,33},{97,1},{2,98}... | collective-permute-start | bytes 1572872 | tf_op jit(solution)/shard_map/ppermute | solution.py:340
  75.8 28.1 %collective-permute-start.9 = (bf16[1024,128]{1,0:T(8,128)(2,1)}, bf16[1024,128]{1,0:T(8,128)(2,1)S(1)}, u32[]{:S(2)}, u32[]{:S(2)}) collective-permute-start(bf16[1024,128]{1,0:T(8,128)(2,1)} %get-tuple-element.23), channel_id=1, source_target_pairs={{128,0},{0,128},{129,1},{1,129},{130,2},{2,130},{131,3},{3,131},{1... | collective-permute-start | bytes 786440 | tf_op jit(solution)/shard_map/ppermute | solution.py:39
  77.7 23.1 %copy-start.3 = (f32[4,128,128]{2,1,0:T(8,128)S(1)}, f32[4,128,128]{2,1,0:T(8,128)}, u32[]{:S(2)}) copy-start(f32[4,128,128]{2,1,0:T(8,128)} %get-tuple-element.38.sin) | copy-start | bytes 786436
  77.7 22.4 %collective-permute-start.11 = (bf16[128,512]{1,0:T(8,128)(2,1)}, bf16[128,512]{1,0:T(8,128)(2,1)S(1)}, u32[]{:S(2)}, u32[]{:S(2)}) collective-permute-start(bf16[128,512]{1,0:T(8,128)(2,1)} %get-tuple-element.25), channel_id=1, source_target_pairs={{0,2},{16,18},{32,34},{48,50},{64,66},{80,82},{96,98},{112,114},{1... | collective-permute-start | bytes 393224 | tf_op jit(solution)/shard_map/ppermute | solution.py:393
  86.9 11.4 %copy-start.32 = (bf16[4,128,256]{2,1,0:T(8,128)(2,1)}, bf16[4,128,256]{2,1,0:T(8,128)(2,1)S(1)}, u32[]{:S(2)}) copy-start(bf16[4,128,256]{2,1,0:T(8,128)(2,1)S(1)} %collective-permute-done.4.kv_c) | copy-start | bytes 786436
  86.9 13.1 %copy-start.34 = (bf16[128,512]{1,0:T(8,128)(2,1)S(1)}, bf16[128,512]{1,0:T(8,128)(2,1)}, u32[]{:S(2)}) copy-start(bf16[128,512]{1,0:T(8,128)(2,1)} %get-tuple-element.25) | copy-start | bytes 393220
  106.5 17.5 %collective-permute-start.16 = (bf16[2048,128]{1,0:T(8,128)(2,1)}, bf16[2048,128]{1,0:T(8,128)(2,1)}, u32[]{:S(2)}, u32[]{:S(2)}) collective-permute-start(bf16[2048,128]{1,0:T(8,128)(2,1)} %pad_maximum_fusion), channel_id=1, source_target_pairs={{0,96},{32,64},{64,32},{96,0},{1,97},{33,65},{65,33},{97,1},{2,98}... | collective-permute-start | bytes 1572872 | tf_op jit(solution)/shard_map/ppermute | solution.py:340
  106.6 17.5 %collective-permute-start.15 = (bf16[2048,128]{1,0:T(8,128)(2,1)}, bf16[2048,128]{1,0:T(8,128)(2,1)S(1)}, u32[]{:S(2)}, u32[]{:S(2)}) collective-permute-start(bf16[2048,128]{1,0:T(8,128)(2,1)} %get-tuple-element.28.o_b), channel_id=1, source_target_pairs={{16,0},{0,16},{17,1},{1,17},{18,2},{2,18},{19,3},{3,19},{20,4},{4,... | collective-permute-start | bytes 1572872 | tf_op jit(solution)/shard_map/ppermute | solution.py:39
  106.7 16.7 %collective-permute-start.13 = (bf16[2,128,256]{2,1,0:T(8,128)(2,1)S(1)}, bf16[2,128,256]{2,1,0:T(8,128)(2,1)S(1)}, u32[]{:S(2)}, u32[]{:S(2)}) collective-permute-start(bf16[2,128,256]{2,1,0:T(8,128)(2,1)S(1)} %slice.32), channel_id=1, source_target_pairs={{0,96},{32,64},{64,32},{96,0},{1,97},{33,65},{65,33},{97,1},{2,98}... | collective-permute-start | bytes 393224 | tf_op jit(solution)/shard_map/ppermute | solution.py:340
  108.8 14.6 %collective-permute-start.12 = (bf16[1024,128]{1,0:T(8,128)(2,1)}, bf16[1024,128]{1,0:T(8,128)(2,1)S(1)}, u32[]{:S(2)}, u32[]{:S(2)}) collective-permute-start(bf16[1024,128]{1,0:T(8,128)(2,1)} %get-tuple-element.27.z2), channel_id=1, source_target_pairs={{16,0},{0,16},{17,1},{1,17},{18,2},{2,18},{19,3},{3,19},{20,4},{4,... | collective-permute-start | bytes 786440 | tf_op jit(solution)/shard_map/ppermute | solution.py:39
  109.0 13.6 %collective-permute-start.17 = (bf16[128,512]{1,0:T(8,128)(2,1)}, bf16[128,512]{1,0:T(8,128)(2,1)S(1)}, u32[]{:S(2)}, u32[]{:S(2)}) collective-permute-start(bf16[128,512]{1,0:T(8,128)(2,1)} %get-tuple-element.29), channel_id=1, source_target_pairs={{0,1},{2,3},{16,17},{18,19},{32,33},{34,35},{48,49},{50,51},{64,65... | collective-permute-start | bytes 393224 | tf_op jit(solution)/shard_map/ppermute | solution.py:393
  111.2 11.4 %copy-start.37 = (bf16[128,512]{1,0:T(8,128)(2,1)S(1)}, bf16[128,512]{1,0:T(8,128)(2,1)}, u32[]{:S(2)}) copy-start(bf16[128,512]{1,0:T(8,128)(2,1)} %get-tuple-element.29) | copy-start | bytes 393220
  124.9 12.3 %collective-permute-start.18 = (bf16[2048,128]{1,0:T(8,128)(2,1)}, bf16[2048,128]{1,0:T(8,128)(2,1)S(1)}, u32[]{:S(2)}, u32[]{:S(2)}) collective-permute-start(bf16[2048,128]{1,0:T(8,128)(2,1)} %get-tuple-element.30.o_zb), channel_id=1, source_target_pairs={{16,0},{0,16},{17,1},{1,17},{18,2},{2,18},{19,3},{3,19},{20,4},{4,... | collective-permute-start | bytes 1572872 | tf_op jit(solution)/shard_map/ppermute | solution.py:39
  125.2 11.4 %collective-permute-start.19 = (bf16[128,512]{1,0:T(8,128)(2,1)}, bf16[128,512]{1,0:T(8,128)(2,1)S(1)}, u32[]{:S(2)}, u32[]{:S(2)}) collective-permute-start(bf16[128,512]{1,0:T(8,128)(2,1)} %get-tuple-element.31), channel_id=1, source_target_pairs={{0,4},{1,5},{2,6},{3,7},{16,20},{17,21},{18,22},{19,23},{32,36},{3... | collective-permute-start | bytes 393224 | tf_op jit(solution)/shard_map/ppermute | solution.py:393
  127.1 9.5 %collective-permute-start.20 = (bf16[128,512]{1,0:T(8,128)(2,1)}, bf16[128,512]{1,0:T(8,128)(2,1)S(1)}, u32[]{:S(2)}, u32[]{:S(2)}) collective-permute-start(bf16[128,512]{1,0:T(8,128)(2,1)} %get-tuple-element.31), channel_id=1, source_target_pairs={{0,8},{1,9},{2,10},{3,11},{16,24},{17,25},{18,26},{19,27},{32,40},... | collective-permute-start | bytes 393224 | tf_op jit(solution)/shard_map/ppermute | solution.py:393
  129.3 7.3 %collective-permute-start.21 = (bf16[128,512]{1,0:T(8,128)(2,1)}, bf16[128,512]{1,0:T(8,128)(2,1)S(1)}, u32[]{:S(2)}, u32[]{:S(2)}) collective-permute-start(bf16[128,512]{1,0:T(8,128)(2,1)} %get-tuple-element.31), channel_id=1, source_target_pairs={{0,12},{1,13},{2,14},{3,15},{16,28},{17,29},{18,30},{19,31},{32,44... | collective-permute-start | bytes 393224 | tf_op jit(solution)/shard_map/ppermute | solution.py:393
  131.5 5.7 %collective-permute-start.14 = (bf16[2,128,256]{2,1,0:T(8,128)(2,1)S(1)}, bf16[2,128,256]{2,1,0:T(8,128)(2,1)S(1)}, u32[]{:S(2)}, u32[]{:S(2)}) collective-permute-start(bf16[2,128,256]{2,1,0:T(8,128)(2,1)S(1)} %slice.33), channel_id=1, source_target_pairs={{0,96},{32,64},{64,32},{96,0},{1,97},{33,65},{65,33},{97,1},{2,98}... | collective-permute-start | bytes 393224 | tf_op jit(solution)/shard_map/ppermute | solution.py:340
  139.5 19.7 %collective-permute-start.22 = (bf16[128,2048]{1,0:T(8,128)(2,1)S(1)}, bf16[128,2048]{1,0:T(8,128)(2,1)S(1)}, u32[]{:S(2)}, u32[]{:S(2)}) collective-permute-start(bf16[128,2048]{1,0:T(8,128)(2,1)S(1)} %get-tuple-element.32), channel_id=1, source_target_pairs={{0,33},{32,1},{64,97},{96,65},{1,34},{33,2},{65,98},{97,66},{2,35}... | collective-permute-start | bytes 1572872 | tf_op jit(solution)/shard_map/ppermute | solution.py:419
  140.5 31.0 %collective-permute-start.23 = (bf16[128,2048]{1,0:T(8,128)(2,1)S(1)}, bf16[128,2048]{1,0:T(8,128)(2,1)S(1)}, u32[]{:S(2)}, u32[]{:S(2)}) collective-permute-start(bf16[128,2048]{1,0:T(8,128)(2,1)S(1)} %get-tuple-element.33), channel_id=1, source_target_pairs={{0,1},{1,2},{2,3},{3,4},{4,5},{5,6},{6,7},{7,8},{8,9},{9,10},{10,1... | collective-permute-start | bytes 1572872 | tf_op jit(solution)/shard_map/ppermute | solution.py:419
  (33 other events, 80.2 us)
